TPU v7x, 256 devices: a whole 4x4x8 slice. The times are simulated.
256 devices in a mesh: space: 256 (over z, x, y, core).
Axes of the slice: x: 4, y: 4, z: 8, core: 2. Of those that a mesh axis runs over, the one named last changes fastest.
Arguments:
- panel: float32 [129, 4194304], P(None, 'space'), as said below
- eig_table: float32 [128, 128], replicated, may hold values from -0.5 to 0.5
- mode_index: int32 [16], replicated, may hold values from 0 to 127
- mode_coef: float32 [16], replicated, may hold values from -4 to 4
Outputs:
- modes: float32 [16, 4194304], P(None, 'space')
- operator: float32 [128, 128], replicated
- first_factor: float32 [128, 128], replicated
Inputs may be any that keep to these rules, and one draw needn't show every extreme that they name: `mode_index`: each entry names a column of eig_table; entries may repeat. `panel`: Real-valued snapshots whose rows have full rank over the grid.
All inputs are finite; a program needn't handle non-finite values.
Results may differ from a plain program's by a relative error of at most 0.00035.
Values sent between devices are 32-bit elements; how exact they have to be, the bound alone decides.
No kernel may reach another device: no remote copies, remote signals or barrier semaphores. Data moves between devices by JAX's collectives and lax.ppermute only.
A program may use at most 128 MiB of HBM per device.

v0:
```python
import functools

import jax
import jax.numpy as jnp
from jax import lax
from jax.experimental import pallas as pl
from jax.experimental.pallas import tpu as pltpu
from jax.sharding import PartitionSpec as P

HIGH = lax.Precision.HIGHEST
F32 = jnp.float32
BF16 = jnp.bfloat16
NT = (((1,), (1,)), ((), ()))
NN = (((1,), (0,)), ((), ()))
TN = (((0,), (0,)), ((), ()))
HALF = 40
LIMIT = 60 * 1024 * 1024


def dot(a, b, dims, precision=None):
    return lax.dot_general(a, b, dims, precision=precision, preferred_element_type=F32)


def two_sum(a, b):
    total = a + b
    other = total - a
    return total, (a - (total - other)) + (b - other)


def split3(x):
    high = x.astype(BF16)
    rest = x - high.astype(F32)
    mid = rest.astype(BF16)
    return high, mid, (rest - mid.astype(F32)).astype(BF16)


def iota(shape, axis):
    return lax.broadcasted_iota(jnp.int32, shape, axis)


def gram_body(chunk, part, panel_ref, kept_ref, sent_ref, x_ref, high_ref, low_ref, cross_ref, mid_ref, last_ref, sems):
    count = panel_ref.shape[1] // chunk
    for index in range(count):
        fetch(panel_ref, x_ref, sems, chunk, index).start()
    for ref in (high_ref, low_ref, cross_ref, mid_ref, last_ref):
        ref[...] = jnp.zeros_like(ref)

    def step(index, carry):
        fetch(panel_ref, x_ref, sems, chunk, index).wait()
        for start in range(0, chunk, part):
            at = pl.ds(pl.multiple_of(index * chunk + start, part), part)
            x = x_ref[0:128, at]
            high, mid, low = split3(x)
            main = dot(jnp.concatenate([high, low], axis=0), jnp.concatenate([high, mid], axis=0), NT)
            total, rest = two_sum(high_ref[...], main[:128, :128])
            high_ref[...] = total
            low_ref[...] += rest
            cross_ref[...] += main[:128, 128:] + (main[128:, :128] + main[128:, 128:])
            mid_ref[...] += dot(mid, mid, NT)
            end = x_ref[128:129, at]
            partial = x[:, 0:128] * end[:, 0:128]
            for tile in range(128, part, 128):
                partial = partial + x[:, tile : tile + 128] * end[:, tile : tile + 128]
            last_ref[...] += partial
        return carry

    lax.fori_loop(0, count, step, 0)
    cross = cross_ref[...]
    rest = low_ref[...] + (mid_ref[...] + (cross + cross.T))
    high, low = two_sum(high_ref[...], rest)
    turned = last_ref[...].T
    end_high = turned[0:8]
    end_low = jnp.zeros_like(end_high)
    for row in range(8, 128, 8):
        end_high, error = two_sum(end_high, turned[row : row + 8])
        end_low = end_low + error
    row_high, row_low = end_high[0:1], end_low[0:1]
    for row in range(1, 8):
        row_high, error = two_sum(row_high, end_high[row : row + 1])
        row_low = row_low + (error + end_low[row : row + 1])
    even = even_core()
    for place, (gram, last) in enumerate(((high, row_high), (low, row_low))):
        packed = pack(gram, last)
        kept_ref[place] = jnp.where(even, packed[:HALF], packed[HALF:])
        sent_ref[place] = jnp.where(even, packed[HALF:], packed[:HALF])


def even_core():
    return lax.axis_index("space") % 2 == 0


def fetch(panel_ref, x_ref, sems, chunk, index):
    at = pl.ds(pl.multiple_of(index * chunk, chunk), chunk)
    return pltpu.make_async_copy(panel_ref.at[:, at], x_ref.at[:, at], sems.at[index])


def pack(gram, last):
    rows, lanes = iota((64, 128), 0), iota((64, 128), 1)
    turned = pltpu.roll(gram[64:128], 64, 1)
    folded = jnp.where(lanes > rows, gram[0:64], jnp.where(lanes < rows, turned, 0.0))
    on_diagonal = iota((128, 128), 0) == iota((128, 128), 1)
    diagonal = jnp.sum(jnp.where(on_diagonal, gram, 0.0), axis=0, keepdims=True)
    return jnp.concatenate([folded, diagonal, last, jnp.zeros((2 * HALF - 66, 128), F32)], axis=0)


def unpack(packed):
    rows, lanes = iota((64, 128), 0), iota((64, 128), 1)
    folded = packed[0:64]
    top = jnp.where(lanes > rows, folded, 0.0)
    turned = pltpu.roll(folded, 64, 1)
    bottom = jnp.where((lanes >= 64) & (lanes - 64 < rows), turned, 0.0)
    half = jnp.concatenate([top, bottom], axis=0)
    on_diagonal = iota((128, 128), 0) == iota((128, 128), 1)
    gram = jnp.where(on_diagonal, packed[64:65], half + half.T)
    return gram, packed[65:66]


def local_gram(panel, chunk=4096, part=1024):
    snaps, columns = panel.shape
    square = pltpu.VMEM((128, 128), F32)
    return pl.pallas_call(
        functools.partial(gram_body, chunk, part),
        in_specs=[pl.BlockSpec(memory_space=pl.ANY)],
        out_shape=[jax.ShapeDtypeStruct((2, HALF, 128), F32)] * 2,
        scratch_shapes=[pltpu.VMEM((snaps, columns), F32)]
        + [square] * 5
        + [pltpu.SemaphoreType.DMA((columns // chunk,))],
        compiler_params=pltpu.CompilerParams(vmem_limit_bytes=LIMIT),
        name="gram",
    )(panel)


def pair_add(a, b):
    total, rest = two_sum(a[0], b[0])
    return jnp.stack([total, (a[1] + b[1]) + rest])


def exchange(x, pairs):
    return lax.ppermute(x, "space", pairs)


def flips(size, step):
    return [(i, i ^ step) for i in range(size)]


def sum_pairs(kept, sent, size):
    half = pair_add(kept, exchange(sent, flips(size, 1)))
    for step in (2, 8):
        first = exchange(half, flips(size, step))
        second = exchange(half, flips(size, 2 * step))
        third = exchange(half, flips(size, 3 * step))
        half = pair_add(pair_add(half, first), pair_add(second, third))
    half = pair_add(half, exchange(half, flips(size, 32)))
    before = exchange(half, [(i, (i + 64) % size) for i in range(size)])
    after = exchange(half, [(i, (i - 64) % size) for i in range(size)])
    across = exchange(half, flips(size, 160))
    half = pair_add(pair_add(half, across), pair_add(before, after))
    return half, exchange(half, flips(size, 1))


def power_scale(square):
    scale = jnp.ones_like(square)
    inverse = jnp.ones_like(square)
    for k in (32, 16, 8, 4, 2, 1):
        big = square >= 4.0**k
        square = jnp.where(big, square * 4.0**-k, square)
        scale = jnp.where(big, scale * 2.0**-k, scale)
        inverse = jnp.where(big, inverse * 2.0**k, inverse)
    for k in (32, 16, 8, 4, 2, 1):
        small = square < 4.0 ** (1 - k)
        square = jnp.where(small, square * 4.0**k, square)
        scale = jnp.where(small, scale * 2.0**k, scale)
        inverse = jnp.where(small, inverse * 2.0**-k, inverse)
    return scale, inverse


def slices(high, low, unit, count):
    out = []
    rest = high
    for index in range(count):
        if index == 2 and low is not None:
            rest = rest + low
        magic = 1.5 * 2.0**23 * unit * 2.0 ** (-9 * index)
        piece = (rest + magic) - magic
        rest = rest - piece
        out.append(piece)
    return out


def add_levels(levels):
    total, rest = two_sum(levels[0], levels[1])
    for level in levels[2:4]:
        total, error = two_sum(total, level)
        rest = rest + error
    for level in levels[4:]:
        rest = rest + level
    return two_sum(total, rest)


def factor(matrix, size=16):
    count = 128 // size
    work = [matrix[size * i : size * i + size] for i in range(count)]
    lanes, rows = iota((size, 128), 1), iota((size, 128), 0)
    extra = [jnp.where(lanes == rows + size * i, 1.0, 0.0).astype(F32) for i in range(count)]
    upper, inverse = [], []
    for block in range(count):
        at = size * block
        wide, carried = work[block], extra[block]
        columns = [jnp.broadcast_to(wide[:, at + k : at + k + 1], (size, 128)) for k in range(size)]
        pivots = jnp.ones((size, 128), F32)
        for j in range(size):
            pivot = columns[j][j : j + 1]
            pivots = jnp.where(rows == j, jnp.broadcast_to(pivot, (size, 128)), pivots)
            if j == size - 1:
                break
            ratio = jnp.where(rows > j, columns[j] * jnp.broadcast_to(1.0 / pivot, (size, 128)), 0.0)
            for k in range(j + 1, size):
                columns[k] = columns[k] - ratio * jnp.broadcast_to(columns[k][j : j + 1], (size, 128))
            wide = wide - ratio * jnp.broadcast_to(wide[j : j + 1], (size, 128))
            carried = carried - ratio * jnp.broadcast_to(carried[j : j + 1], (size, 128))
        root = lax.rsqrt(pivots)
        root = root * (1.5 - 0.5 * pivots * root * root)
        wide = jnp.where(lanes >= rows + at, wide * root, 0.0)
        carried = carried * root
        upper.append(wide)
        inverse.append(carried)
        if block < count - 1:
            left = split3(wide)
            right = split3(jnp.concatenate([wide, carried], axis=1))
            order = ((0, 0), (0, 1), (1, 0), (1, 1), (0, 2), (2, 0))
            update = dot(
                jnp.concatenate([left[i] for i, _ in order], axis=0),
                jnp.concatenate([right[j] for _, j in order], axis=0),
                TN,
            )
            for later in range(block + 1, count):
                at = size * later
                work[later] = work[later] - update[at : at + size, :128]
                extra[later] = extra[later] - update[at : at + size, 128:]
    return jnp.concatenate(upper, axis=0), jnp.concatenate(inverse, axis=0)


def finish_body(
    root,
    chunk,
    out_chunk,
    mine_ref,
    other_ref,
    table_ref,
    index_ref,
    coef_ref,
    panel_ref,
    modes_ref,
    operator_ref,
    factor_ref,
    x_ref,
    y_ref,
    shift_ref,
    in_sems,
    out_sems,
):
    columns = panel_ref.shape[1]
    for index in range(columns // chunk):
        fetch(panel_ref, x_ref, in_sems, chunk, index).start()
    even = even_core()
    mine, other = mine_ref[...], other_ref[...]
    packed = jnp.concatenate([jnp.where(even, mine, other), jnp.where(even, other, mine)], axis=1)
    gram_high, last_high = unpack(packed[0])
    gram_low, last_low = unpack(packed[1])
    gram_high, gram_low = two_sum(gram_high, gram_low)
    last_high, last_low = two_sum(last_high, last_low)
    on_diagonal = iota((128, 128), 0) == iota((128, 128), 1)
    diagonal = jnp.sum(jnp.where(on_diagonal, gram_high, 0.0), axis=0, keepdims=True)
    scale, unscale = power_scale(diagonal)
    scale_wide = jnp.broadcast_to(scale, (128, 128))
    scale_tall = scale_wide.T
    gram_high = gram_high * scale_wide * scale_tall
    gram_low = gram_low * scale_wide * scale_tall
    last_high = last_high * scale
    last_low = last_low * scale
    biggest = jnp.max(jnp.abs(last_high), axis=1, keepdims=True)
    last_scale, last_unscale = power_scale(jnp.broadcast_to(biggest * biggest, (1, 128)))
    last_high = last_high * last_scale
    last_low = last_low * last_scale

    upper, lower_inverse = factor(gram_high)
    factor_ref[...] = upper * (unscale * (1.0 / root))

    norms = jnp.sum(lower_inverse * lower_inverse, axis=1, keepdims=True)
    row_scale, _ = power_scale(jnp.broadcast_to(norms, (128, 128)))
    y_one, y_two = slices(lower_inverse * row_scale, None, 2.0**-7, 2)
    first = y_one + y_two
    y_both = jnp.concatenate([y_one, y_two], axis=0).astype(BF16)

    blank = jnp.zeros((7, 128), F32)
    whole_high = jnp.concatenate([gram_high, last_high, blank], axis=0)
    whole_low = jnp.concatenate([gram_low, last_low, blank], axis=0)
    g = [piece.astype(BF16) for piece in slices(whole_high, whole_low, 2.0**-6, 4)]
    p = [dot(piece, y_both, NT) for piece in g]
    one = [piece[:, :128] for piece in p]
    two = [piece[:, 128:] for piece in p]
    t_high, t_low = add_levels(
        [one[0], one[1] + two[0], one[2] + two[1], one[3] + two[2], two[3]]
    )

    norms = jnp.sum(t_high[:128] * t_high[:128], axis=0, keepdims=True)
    column_scale, column_unscale = power_scale(norms)
    t = slices(t_high[:128] * column_scale, t_low[:128] * column_scale, 2.0**-7, 4)
    t_all = jnp.concatenate([piece.astype(BF16) for piece in t], axis=1)
    s = dot(y_both, t_all, NN)
    one = [s[:128, 128 * k : 128 * k + 128] for k in range(4)]
    two = [s[128:, 128 * k : 128 * k + 128] for k in range(4)]
    s_high, s_low = add_levels(
        [one[0], one[1] + two[0], one[2] + two[1], one[3] + two[2], two[3]]
    )
    _, second = factor((s_high + s_low) * column_unscale)

    whole = dot(second, first, NN, HIGH)
    shift_ref[...] = t_high
    z = shift_ref[1:129]
    following = jnp.where(iota((1, 128), 1) == 127, last_unscale, pltpu.roll(unscale, 127, 1))
    h = dot(whole * (scale * following), z, NN, HIGH)
    operator_ref[...] = dot(second, h, NT, HIGH)

    rows = iota((16, 128), 0)
    index, coef = jnp.zeros((16, 128), jnp.int32), jnp.zeros((16, 128), F32)
    for mode in range(16):
        index = jnp.where(rows == mode, index_ref[mode], index)
        coef = jnp.where(rows == mode, coef_ref[mode], coef)
    onehot = (iota((16, 128), 1) == index).astype(F32)
    chosen = dot(onehot, table_ref[...], NT, HIGH)
    comb = dot(chosen, whole, NN, HIGH) * scale * (coef * root)

    for index in range(columns // chunk):
        fetch(panel_ref, x_ref, in_sems, chunk, index).wait()
    shifted = jnp.where(iota(comb.shape, 1) == 0, 0.0, pltpu.roll(comb, 1, 1))
    c = split3(shifted)
    left = jnp.concatenate(
        [
            jnp.concatenate([c[0], c[1]], axis=1),
            jnp.concatenate([c[1], c[0]], axis=1),
            jnp.concatenate([c[2], jnp.zeros_like(c[2])], axis=1),
        ],
        axis=0,
    )

    def send(index):
        at = pl.ds(pl.multiple_of(index * out_chunk, out_chunk), out_chunk)
        return pltpu.make_async_copy(y_ref.at[:, at], modes_ref.at[:, at], out_sems.at[index])

    def step(index, carry):
        at = pl.ds(pl.multiple_of(index * out_chunk, out_chunk), out_chunk)
        x_high, x_mid, x_low = split3(x_ref[0:128, at])
        main = dot(left, jnp.concatenate([x_high, x_mid], axis=0), NN)
        side = dot(c[0], x_low, NN)
        end = comb[:, 127:128] * x_ref[128:129, at]
        y_ref[:, at] = (main[0:16] + end) + (main[16:32] + (main[32:48] + side))
        send(index).start()
        return carry

    lax.fori_loop(0, columns // out_chunk, step, 0)
    for index in range(columns // out_chunk):
        send(index).wait()


def finish(mine, other, table, index, coef, panel, total_rows, chunk=4096, out_chunk=2048):
    root = float(total_rows) ** 0.5
    modes = index.shape[0]
    snaps, columns = panel.shape
    whole = pl.BlockSpec(memory_space=pltpu.VMEM)
    remote = pl.BlockSpec(memory_space=pl.ANY)
    scalars = pl.BlockSpec(memory_space=pltpu.SMEM)
    return pl.pallas_call(
        functools.partial(finish_body, root, chunk, out_chunk),
        in_specs=[whole] * 3 + [scalars] * 2 + [remote],
        out_specs=[remote, whole, whole],
        out_shape=[
            jax.ShapeDtypeStruct((modes, columns), F32),
            jax.ShapeDtypeStruct((128, 128), F32),
            jax.ShapeDtypeStruct((128, 128), F32),
        ],
        scratch_shapes=[
            pltpu.VMEM((snaps, columns), F32),
            pltpu.VMEM((modes, columns), F32),
            pltpu.VMEM((136, 128), F32),
            pltpu.SemaphoreType.DMA((columns // chunk,)),
            pltpu.SemaphoreType.DMA((columns // out_chunk,)),
        ],
        compiler_params=pltpu.CompilerParams(vmem_limit_bytes=LIMIT),
        name="finish",
    )(mine, other, table, index, coef, panel)


def local(size, panel, eig_table, mode_index, mode_coef):
    mine, other = sum_pairs(*local_gram(panel), size)
    return tuple(finish(mine, other, eig_table, mode_index, mode_coef, panel, panel.shape[1] * size))


def solution(mesh):
    return jax.shard_map(
        functools.partial(local, mesh.shape["space"]),
        mesh=mesh,
        in_specs=(P(None, "space"), P(), P(), P()),
        out_specs=(P(None, "space"), P(), P()),
        check_vma=False,
    )
```

profile of v0, /device:TPU:1, one launch (start us, length us, event | category | flops | bytes accessed | tf_op | source)
XLA Modules:
  0.0 65.3 jit_solution(16366310518737257380)
XLA Ops:
  0.6 6.7 %gram.1 = (f32[2,40,128]{2,1,0:T(8,128)}, f32[2,40,128]{2,1,0:T(8,128)}) custom-call(f32[129,16384]{1,0:T(8,128)} %panel_ref.3), custom_call_target="tpu_custom_call" | custom-call | tf_op jit(solution)/shard_map/gram/pallas_call | solution.py:121
  7.3 3.3 %collective-permute-start = (f32[2,40,128]{2,1,0:T(8,128)}, f32[2,40,128]{2,1,0:T(8,128)S(1)}, u32[]{:S(2)}, u32[]{:S(2)}) collective-permute-start(f32[2,40,128]{2,1,0:T(8,128)} %get-tuple-element.6), channel_id=1, source_target_pairs={{0,1},{1,0},{2,3},{3,2},{4,5},{5,4},{6,7},{7,6},{8,9},{9,8},{10,11... | collective-permute-start | bytes 122888 | tf_op jit(solution)/shard_map/ppermute | solution.py:139
  10.7 1.1 %collective-permute-done = f32[2,40,128]{2,1,0:T(8,128)S(1)} collective-permute-done((f32[2,40,128]{2,1,0:T(8,128)}, f32[2,40,128]{2,1,0:T(8,128)S(1)}, u32[]{:S(2)}, u32[]{:S(2)}) %collective-permute-start) | collective-permute-done | bytes 40992 | tf_op jit(solution)/shard_map/ppermute | solution.py:139
  11.7 0.8 %fusion.13 = (f32[1,40,128]{2,1,0:T(8,128)S(1)}, f32[1,40,128]{2,1,0:T(8,128)S(1)}) fusion(f32[2,40,128]{2,1,0:T(8,128)S(1)} %collective-permute-done, f32[2,40,128]{2,1,0:T(8,128)} %get-tuple-element.5), kind=kLoop, calls=%fused_computation.26 | loop fusion | flops 40960 | bytes 122880 | tf_op jit(solution)/shard_map/add | solution.py:135
  12.5 1.1 %collective-permute-start.3 = (f32[2,40,128]{2,1,0:T(8,128)S(1)}, f32[2,40,128]{2,1,0:T(8,128)S(1)}, u32[]{:S(2)}, u32[]{:S(2)}) collective-permute-start(f32[2,40,128]{2,1,0:T(8,128)S(1)} %pad_maximum_fusion), channel_id=1, source_target_pairs={{0,6},{1,7},{2,4},{3,5},{4,2},{5,3},{6,0},{7,1},{8,14},{9,15},{10,... | collective-permute-start | bytes 122888 | tf_op jit(solution)/shard_map/ppermute | solution.py:139
  13.6 0.3 collective-permute-start.2
  13.9 1.9 %collective-permute-start.1 = (f32[2,40,128]{2,1,0:T(8,128)S(1)}, f32[2,40,128]{2,1,0:T(8,128)S(1)}, u32[]{:S(2)}, u32[]{:S(2)}) collective-permute-start(f32[2,40,128]{2,1,0:T(8,128)S(1)} %pad_maximum_fusion), channel_id=1, source_target_pairs={{0,2},{1,3},{2,0},{3,1},{4,6},{5,7},{6,4},{7,5},{8,10},{9,11},{10,... | collective-permute-start | bytes 122888 | tf_op jit(solution)/shard_map/ppermute | solution.py:139
  15.8 0.8 %collective-permute-done.3 = f32[2,40,128]{2,1,0:T(8,128)S(1)} collective-permute-done((f32[2,40,128]{2,1,0:T(8,128)S(1)}, f32[2,40,128]{2,1,0:T(8,128)S(1)}, u32[]{:S(2)}, u32[]{:S(2)}) %collective-permute-start.3) | collective-permute-done | bytes 40992 | tf_op jit(solution)/shard_map/ppermute | solution.py:139
  16.7 1.3 %collective-permute-done.2 = f32[2,40,128]{2,1,0:T(8,128)S(1)} collective-permute-done((f32[2,40,128]{2,1,0:T(8,128)S(1)}, f32[2,40,128]{2,1,0:T(8,128)S(1)}, u32[]{:S(2)}, u32[]{:S(2)}) %collective-permute-start.2) | collective-permute-done | bytes 40992 | tf_op jit(solution)/shard_map/ppermute | solution.py:139
  18.0 0.0 collective-permute-done.1
  18.0 2.6 %collective-permute-start.6 = (f32[2,40,128]{2,1,0:T(8,128)S(1)}, f32[2,40,128]{2,1,0:T(8,128)S(1)}, u32[]{:S(2)}, u32[]{:S(2)}) collective-permute-start(f32[2,40,128]{2,1,0:T(8,128)S(1)} %pad_maximum_fusion.1), channel_id=1, source_target_pairs={{0,24},{1,25},{2,26},{3,27},{4,28},{5,29},{6,30},{7,31},{8,16},{9,... | collective-permute-start | bytes 122888 | tf_op jit(solution)/shard_map/ppermute | solution.py:139
  20.6 0.5 collective-permute-start.5
  21.1 0.3 collective-permute-start.4
  21.3 0.8 %collective-permute-done.6 = f32[2,40,128]{2,1,0:T(8,128)S(1)} collective-permute-done((f32[2,40,128]{2,1,0:T(8,128)S(1)}, f32[2,40,128]{2,1,0:T(8,128)S(1)}, u32[]{:S(2)}, u32[]{:S(2)}) %collective-permute-start.6) | collective-permute-done | bytes 40992 | tf_op jit(solution)/shard_map/ppermute | solution.py:139
  22.2 2.8 %collective-permute-done.5 = f32[2,40,128]{2,1,0:T(8,128)S(1)} collective-permute-done((f32[2,40,128]{2,1,0:T(8,128)S(1)}, f32[2,40,128]{2,1,0:T(8,128)S(1)}, u32[]{:S(2)}, u32[]{:S(2)}) %collective-permute-start.5) | collective-permute-done | bytes 40992 | tf_op jit(solution)/shard_map/ppermute | solution.py:139
  24.9 0.0 collective-permute-done.4
  25.0 1.7 %collective-permute-start.7 = (f32[2,40,128]{2,1,0:T(8,128)S(1)}, f32[2,40,128]{2,1,0:T(8,128)S(1)}, u32[]{:S(2)}, u32[]{:S(2)}) collective-permute-start(f32[2,40,128]{2,1,0:T(8,128)S(1)} %pad_maximum_fusion.2), channel_id=1, source_target_pairs={{0,32},{1,33},{2,34},{3,35},{4,36},{5,37},{6,38},{7,39},{8,40},{9,... | collective-permute-start | bytes 122888 | tf_op jit(solution)/shard_map/ppermute | solution.py:139
  26.7 1.4 %collective-permute-done.7 = f32[2,40,128]{2,1,0:T(8,128)S(1)} collective-permute-done((f32[2,40,128]{2,1,0:T(8,128)S(1)}, f32[2,40,128]{2,1,0:T(8,128)S(1)}, u32[]{:S(2)}, u32[]{:S(2)}) %collective-permute-start.7) | collective-permute-done | bytes 40992 | tf_op jit(solution)/shard_map/ppermute | solution.py:139
  28.1 5.9 %collective-permute-start.10 = (f32[2,40,128]{2,1,0:T(8,128)S(1)}, f32[2,40,128]{2,1,0:T(8,128)S(1)}, u32[]{:S(2)}, u32[]{:S(2)}) collective-permute-start(f32[2,40,128]{2,1,0:T(8,128)S(1)} %pad_maximum_fusion.3), channel_id=1, source_target_pairs={{0,192},{1,193},{2,194},{3,195},{4,196},{5,197},{6,198},{7,199},{8... | collective-permute-start | bytes 122888 | tf_op jit(solution)/shard_map/ppermute | solution.py:139
  34.0 0.0 collective-permute-start.9
  34.0 2.8 %collective-permute-start.8 = (f32[2,40,128]{2,1,0:T(8,128)S(1)}, f32[2,40,128]{2,1,0:T(8,128)S(1)}, u32[]{:S(2)}, u32[]{:S(2)}) collective-permute-start(f32[2,40,128]{2,1,0:T(8,128)S(1)} %pad_maximum_fusion.3), channel_id=1, source_target_pairs={{0,160},{1,161},{2,162},{3,163},{4,164},{5,165},{6,166},{7,167},{8... | collective-permute-start | bytes 122888 | tf_op jit(solution)/shard_map/ppermute | solution.py:139
  36.9 0.0 collective-permute-done.10
  36.9 2.2 %collective-permute-done.9 = f32[2,40,128]{2,1,0:T(8,128)S(1)} collective-permute-done((f32[2,40,128]{2,1,0:T(8,128)S(1)}, f32[2,40,128]{2,1,0:T(8,128)S(1)}, u32[]{:S(2)}, u32[]{:S(2)}) %collective-permute-start.9) | collective-permute-done | bytes 40992 | tf_op jit(solution)/shard_map/ppermute | solution.py:139
  39.0 0.9 %collective-permute-done.8 = f32[2,40,128]{2,1,0:T(8,128)S(1)} collective-permute-done((f32[2,40,128]{2,1,0:T(8,128)S(1)}, f32[2,40,128]{2,1,0:T(8,128)S(1)}, u32[]{:S(2)}, u32[]{:S(2)}) %collective-permute-start.8) | collective-permute-done | bytes 40992 | tf_op jit(solution)/shard_map/ppermute | solution.py:139
  39.9 0.0 copy-start
  40.0 6.2 %collective-permute-start.11 = (f32[2,40,128]{2,1,0:T(8,128)S(1)}, f32[2,40,128]{2,1,0:T(8,128)S(1)}, u32[]{:S(2)}, u32[]{:S(2)}) collective-permute-start(f32[2,40,128]{2,1,0:T(8,128)S(1)} %pad_maximum_fusion.4.mine_ref), channel_id=1, source_target_pairs={{0,1},{1,0},{2,3},{3,2},{4,5},{5,4},{6,7},{7,6},{8,9},{9,8},{10,11... | collective-permute-start | bytes 122888 | tf_op jit(solution)/shard_map/ppermute | solution.py:139
  46.2 0.9 %collective-permute-done.11.other_ref = f32[2,40,128]{2,1,0:T(8,128)S(1)} collective-permute-done((f32[2,40,128]{2,1,0:T(8,128)S(1)}, f32[2,40,128]{2,1,0:T(8,128)S(1)}, u32[]{:S(2)}, u32[]{:S(2)}) %collective-permute-start.11) | collective-permute-done | bytes 40992 | tf_op jit(solution)/shard_map/ppermute | solution.py:139
  47.1 0.0 copy-done
  47.1 0.0 copy-start.1
  47.1 0.6 copy-done.1
  47.7 17.5 %finish.1 = (f32[16,16384]{1,0:T(8,128)}, f32[128,128]{1,0:T(8,128)}, f32[128,128]{1,0:T(8,128)}) custom-call(f32[2,40,128]{2,1,0:T(8,128)} %copy-done, f32[2,40,128]{2,1,0:T(8,128)} %copy-done.1, f32[128,128]{1,0:T(8,128)} %table_ref.1, s32[16]{0:T(128)} %index_ref.1, f32[16]{0:T(128)} %coef_ref.1, f32[129,16384]{1,0:T(8,128)} %panel_ref.3), custom_call_target="tpu_custom_call" | custom-call | tf_op jit(solution)/shard_map/finish/pallas_call | solution.py:373
  (9 shorter events, 0.1 us)
Async XLA Ops:
  7.3 4.4 %collective-permute-start = (f32[2,40,128]{2,1,0:T(8,128)}, f32[2,40,128]{2,1,0:T(8,128)S(1)}, u32[]{:S(2)}, u32[]{:S(2)}) collective-permute-start(f32[2,40,128]{2,1,0:T(8,128)} %get-tuple-element.6), channel_id=1, source_target_pairs={{0,1},{1,0},{2,3},{3,2},{4,5},{5,4},{6,7},{7,6},{8,9},{9,8},{10,11... | collective-permute-start | bytes 122888 | tf_op jit(solution)/shard_map/ppermute | solution.py:139
  12.5 4.2 %collective-permute-start.3 = (f32[2,40,128]{2,1,0:T(8,128)S(1)}, f32[2,40,128]{2,1,0:T(8,128)S(1)}, u32[]{:S(2)}, u32[]{:S(2)}) collective-permute-start(f32[2,40,128]{2,1,0:T(8,128)S(1)} %pad_maximum_fusion), channel_id=1, source_target_pairs={{0,6},{1,7},{2,4},{3,5},{4,2},{5,3},{6,0},{7,1},{8,14},{9,15},{10,... | collective-permute-start | bytes 122888 | tf_op jit(solution)/shard_map/ppermute | solution.py:139
  13.6 4.4 %collective-permute-start.2 = (f32[2,40,128]{2,1,0:T(8,128)S(1)}, f32[2,40,128]{2,1,0:T(8,128)S(1)}, u32[]{:S(2)}, u32[]{:S(2)}) collective-permute-start(f32[2,40,128]{2,1,0:T(8,128)S(1)} %pad_maximum_fusion), channel_id=1, source_target_pairs={{0,4},{1,5},{2,6},{3,7},{4,0},{5,1},{6,2},{7,3},{8,12},{9,13},{10,... | collective-permute-start | bytes 122888 | tf_op jit(solution)/shard_map/ppermute | solution.py:139
  13.9 4.0 %collective-permute-start.1 = (f32[2,40,128]{2,1,0:T(8,128)S(1)}, f32[2,40,128]{2,1,0:T(8,128)S(1)}, u32[]{:S(2)}, u32[]{:S(2)}) collective-permute-start(f32[2,40,128]{2,1,0:T(8,128)S(1)} %pad_maximum_fusion), channel_id=1, source_target_pairs={{0,2},{1,3},{2,0},{3,1},{4,6},{5,7},{6,4},{7,5},{8,10},{9,11},{10,... | collective-permute-start | bytes 122888 | tf_op jit(solution)/shard_map/ppermute | solution.py:139
  18.0 4.2 %collective-permute-start.6 = (f32[2,40,128]{2,1,0:T(8,128)S(1)}, f32[2,40,128]{2,1,0:T(8,128)S(1)}, u32[]{:S(2)}, u32[]{:S(2)}) collective-permute-start(f32[2,40,128]{2,1,0:T(8,128)S(1)} %pad_maximum_fusion.1), channel_id=1, source_target_pairs={{0,24},{1,25},{2,26},{3,27},{4,28},{5,29},{6,30},{7,31},{8,16},{9,... | collective-permute-start | bytes 122888 | tf_op jit(solution)/shard_map/ppermute | solution.py:139
  20.6 4.4 %collective-permute-start.5 = (f32[2,40,128]{2,1,0:T(8,128)S(1)}, f32[2,40,128]{2,1,0:T(8,128)S(1)}, u32[]{:S(2)}, u32[]{:S(2)}) collective-permute-start(f32[2,40,128]{2,1,0:T(8,128)S(1)} %pad_maximum_fusion.1), channel_id=1, source_target_pairs={{0,16},{1,17},{2,18},{3,19},{4,20},{5,21},{6,22},{7,23},{8,24},{9,... | collective-permute-start | bytes 122888 | tf_op jit(solution)/shard_map/ppermute | solution.py:139
  21.1 3.8 %collective-permute-start.4 = (f32[2,40,128]{2,1,0:T(8,128)S(1)}, f32[2,40,128]{2,1,0:T(8,128)S(1)}, u32[]{:S(2)}, u32[]{:S(2)}) collective-permute-start(f32[2,40,128]{2,1,0:T(8,128)S(1)} %pad_maximum_fusion.1), channel_id=1, source_target_pairs={{0,8},{1,9},{2,10},{3,11},{4,12},{5,13},{6,14},{7,15},{8,0},{9,1},... | collective-permute-start | bytes 122888 | tf_op jit(solution)/shard_map/ppermute | solution.py:139
  25.0 3.1 %collective-permute-start.7 = (f32[2,40,128]{2,1,0:T(8,128)S(1)}, f32[2,40,128]{2,1,0:T(8,128)S(1)}, u32[]{:S(2)}, u32[]{:S(2)}) collective-permute-start(f32[2,40,128]{2,1,0:T(8,128)S(1)} %pad_maximum_fusion.2), channel_id=1, source_target_pairs={{0,32},{1,33},{2,34},{3,35},{4,36},{5,37},{6,38},{7,39},{8,40},{9,... | collective-permute-start | bytes 122888 | tf_op jit(solution)/shard_map/ppermute | solution.py:139
  28.1 8.7 %collective-permute-start.10 = (f32[2,40,128]{2,1,0:T(8,128)S(1)}, f32[2,40,128]{2,1,0:T(8,128)S(1)}, u32[]{:S(2)}, u32[]{:S(2)}) collective-permute-start(f32[2,40,128]{2,1,0:T(8,128)S(1)} %pad_maximum_fusion.3), channel_id=1, source_target_pairs={{0,192},{1,193},{2,194},{3,195},{4,196},{5,197},{6,198},{7,199},{8... | collective-permute-start | bytes 122888 | tf_op jit(solution)/shard_map/ppermute | solution.py:139
  34.0 5.0 %collective-permute-start.9 = (f32[2,40,128]{2,1,0:T(8,128)S(1)}, f32[2,40,128]{2,1,0:T(8,128)S(1)}, u32[]{:S(2)}, u32[]{:S(2)}) collective-permute-start(f32[2,40,128]{2,1,0:T(8,128)S(1)} %pad_maximum_fusion.3), channel_id=1, source_target_pairs={{0,64},{1,65},{2,66},{3,67},{4,68},{5,69},{6,70},{7,71},{8,72},{9,... | collective-permute-start | bytes 122888 | tf_op jit(solution)/shard_map/ppermute | solution.py:139
  34.0 5.9 %collective-permute-start.8 = (f32[2,40,128]{2,1,0:T(8,128)S(1)}, f32[2,40,128]{2,1,0:T(8,128)S(1)}, u32[]{:S(2)}, u32[]{:S(2)}) collective-permute-start(f32[2,40,128]{2,1,0:T(8,128)S(1)} %pad_maximum_fusion.3), channel_id=1, source_target_pairs={{0,160},{1,161},{2,162},{3,163},{4,164},{5,165},{6,166},{7,167},{8... | collective-permute-start | bytes 122888 | tf_op jit(solution)/shard_map/ppermute | solution.py:139
  39.9 7.1 %copy-start = (f32[2,40,128]{2,1,0:T(8,128)}, f32[2,40,128]{2,1,0:T(8,128)S(1)}, u32[]{:S(2)}) copy-start(f32[2,40,128]{2,1,0:T(8,128)S(1)} %pad_maximum_fusion.4.mine_ref) | copy-start | bytes 122884
  40.0 7.1 %collective-permute-start.11 = (f32[2,40,128]{2,1,0:T(8,128)S(1)}, f32[2,40,128]{2,1,0:T(8,128)S(1)}, u32[]{:S(2)}, u32[]{:S(2)}) collective-permute-start(f32[2,40,128]{2,1,0:T(8,128)S(1)} %pad_maximum_fusion.4.mine_ref), channel_id=1, source_target_pairs={{0,1},{1,0},{2,3},{3,2},{4,5},{5,4},{6,7},{7,6},{8,9},{9,8},{10,11... | collective-permute-start | bytes 122888 | tf_op jit(solution)/shard_map/ppermute | solution.py:139
  47.1 0.6 copy-start.1
where the time goes:
time: 65.5 us; the launch traced here: 65.3 us
  starting transfers between devices  26.7 us (41%)
  Pallas kernels  24.1 us (37%)
  waiting for transfers between devices  12.1 us (18%)
  other arithmetic  0.88 us (1%)
  between operations  0.87 us (1%)
    ppermute x12, starting transfers between devices, exchange(): return lax.ppermute(x, 'space', pairs)  26.7 us
    pallas_call x1, Pallas kernels, finish(): pl.pallas_call(functools.partial(finish_body, root, chunk, out_chunk), in...  17.5 us
    ppermute x12, waiting for transfers between devices, exchange(): return lax.ppermute(x, 'space', pairs)  12.1 us
    pallas_call x1, Pallas kernels, local_gram(): pl.pallas_call(functools.partial(gram_body, chunk, part), in_specs=[pl.Bl...  6.69 us
  transfers between devices with their start and end apart: 12, of which 9 were waited for; matrix products, arithmetic and copies ran while one was open for 0% of the time, Pallas kernels for 0%

commit v1 on v0

--- a/solution.py
+++ b/solution.py
@@ -14,7 +14,8 @@
 NN = (((1,), (0,)), ((), ()))
 TN = (((0,), (0,)), ((), ()))
 HALF = 40
-LIMIT = 60 * 1024 * 1024
+GRAM_LIMIT = 50 * 1024 * 1024
+LIMIT = 32 * 1024 * 1024
 
 
 def dot(a, b, dims, precision=None):
@@ -121,11 +122,11 @@
     return pl.pallas_call(
         functools.partial(gram_body, chunk, part),
         in_specs=[pl.BlockSpec(memory_space=pl.ANY)],
-        out_shape=[jax.ShapeDtypeStruct((2, HALF, 128), F32)] * 2,
-        scratch_shapes=[pltpu.VMEM((snaps, columns), F32)]
-        + [square] * 5
+        out_shape=[pltpu.VMEM((2, HALF, 128), F32)] * 2 + [pltpu.VMEM((snaps, columns), F32)],
+        out_specs=[pl.BlockSpec(memory_space=pltpu.VMEM)] * 3,
+        scratch_shapes=[square] * 5
         + [pltpu.SemaphoreType.DMA((columns // chunk,))],
-        compiler_params=pltpu.CompilerParams(vmem_limit_bytes=LIMIT),
+        compiler_params=pltpu.CompilerParams(vmem_limit_bytes=GRAM_LIMIT),
         name="gram",
     )(panel)
 
@@ -242,26 +243,21 @@
 
 def finish_body(
     root,
-    chunk,
     out_chunk,
     mine_ref,
     other_ref,
     table_ref,
     index_ref,
     coef_ref,
-    panel_ref,
+    x_ref,
     modes_ref,
     operator_ref,
     factor_ref,
-    x_ref,
     y_ref,
     shift_ref,
-    in_sems,
     out_sems,
 ):
-    columns = panel_ref.shape[1]
-    for index in range(columns // chunk):
-        fetch(panel_ref, x_ref, in_sems, chunk, index).start()
+    columns = x_ref.shape[1]
     even = even_core()
     mine, other = mine_ref[...], other_ref[...]
     packed = jnp.concatenate([jnp.where(even, mine, other), jnp.where(even, other, mine)], axis=1)
@@ -331,8 +327,6 @@
     chosen = dot(onehot, table_ref[...], NT, HIGH)
     comb = dot(chosen, whole, NN, HIGH) * scale * (coef * root)
 
-    for index in range(columns // chunk):
-        fetch(panel_ref, x_ref, in_sems, chunk, index).wait()
     shifted = jnp.where(iota(comb.shape, 1) == 0, 0.0, pltpu.roll(comb, 1, 1))
     c = split3(shifted)
     left = jnp.concatenate(
@@ -363,16 +357,16 @@
         send(index).wait()
 
 
-def finish(mine, other, table, index, coef, panel, total_rows, chunk=4096, out_chunk=2048):
+def finish(mine, other, table, index, coef, panel, total_rows, out_chunk=2048):
     root = float(total_rows) ** 0.5
     modes = index.shape[0]
-    snaps, columns = panel.shape
+    columns = panel.shape[1]
     whole = pl.BlockSpec(memory_space=pltpu.VMEM)
     remote = pl.BlockSpec(memory_space=pl.ANY)
     scalars = pl.BlockSpec(memory_space=pltpu.SMEM)
     return pl.pallas_call(
-        functools.partial(finish_body, root, chunk, out_chunk),
-        in_specs=[whole] * 3 + [scalars] * 2 + [remote],
+        functools.partial(finish_body, root, out_chunk),
+        in_specs=[whole] * 3 + [scalars] * 2 + [whole],
         out_specs=[remote, whole, whole],
         out_shape=[
             jax.ShapeDtypeStruct((modes, columns), F32),
@@ -380,10 +374,8 @@
             jax.ShapeDtypeStruct((128, 128), F32),
         ],
         scratch_shapes=[
-            pltpu.VMEM((snaps, columns), F32),
             pltpu.VMEM((modes, columns), F32),
             pltpu.VMEM((136, 128), F32),
-            pltpu.SemaphoreType.DMA((columns // chunk,)),
             pltpu.SemaphoreType.DMA((columns // out_chunk,)),
         ],
         compiler_params=pltpu.CompilerParams(vmem_limit_bytes=LIMIT),
@@ -392,8 +384,9 @@
 
 
 def local(size, panel, eig_table, mode_index, mode_coef):
-    mine, other = sum_pairs(*local_gram(panel), size)
-    return tuple(finish(mine, other, eig_table, mode_index, mode_coef, panel, panel.shape[1] * size))
+    kept, sent, held = local_gram(panel)
+    mine, other = sum_pairs(kept, sent, size)
+    return tuple(finish(mine, other, eig_table, mode_index, mode_coef, held, panel.shape[1] * size))
 
 
 def solution(mesh):

time: 65.5 us -> 59.9 us (0.915)
  Pallas kernels: 24.1 us -> 20.2 us
  other arithmetic: 0.88 us -> 0.14 us
    pallas_call x1, Pallas kernels: 17.5 us -> 14.1 us  [finish(): pl.pallas_call(functools.partial(finish_body, root, out_chunk), in_specs=...]
    add x5, other arithmetic: 0.85 us -> 0.11 us  [pair_add(): return jnp.stack([total, a[1] + b[1] + rest])]
where the time goes in v1:
time: 59.9 us; the launch traced here: 59.8 us
  starting transfers between devices  26.7 us (45%)
  Pallas kernels  20.2 us (34%)
  waiting for transfers between devices  11.9 us (20%)
  between operations  0.89 us (1%)
    ppermute x12, starting transfers between devices, exchange(): return lax.ppermute(x, 'space', pairs)  26.7 us
    pallas_call x1, Pallas kernels, finish(): pl.pallas_call(functools.partial(finish_body, root, out_chunk), in_specs=...  14.1 us
    ppermute x12, waiting for transfers between devices, exchange(): return lax.ppermute(x, 'space', pairs)  11.9 us
    pallas_call x1, Pallas kernels, local_gram(): pl.pallas_call(functools.partial(gram_body, chunk, part), in_specs=[pl.Bl...  6.09 us
  transfers between devices with their start and end apart: 12, of which 9 were waited for; matrix products, arithmetic and copies ran while one was open for 0% of the time, Pallas kernels for 0%

profile of v1, /device:TPU:1, one launch (start us, length us, event | category | flops | bytes accessed | tf_op | source)
XLA Modules:
  0.0 59.8 jit_solution(5197808152200509354)
XLA Ops:
  0.6 0.0 copy-start.2
  0.6 0.0 copy-start.1
  0.7 0.0 copy-start
  0.7 6.1 %gram.1 = (f32[2,40,128]{2,1,0:T(8,128)S(1)}, f32[2,40,128]{2,1,0:T(8,128)S(1)}, f32[129,16384]{1,0:T(8,128)S(1)}) custom-call(f32[129,16384]{1,0:T(8,128)} %panel_ref.1), custom_call_target="tpu_custom_call" | custom-call | tf_op jit(solution)/shard_map/gram/pallas_call | solution.py:122
  6.8 3.3 %collective-permute-start = (f32[2,40,128]{2,1,0:T(8,128)S(1)}, f32[2,40,128]{2,1,0:T(8,128)S(1)}, u32[]{:S(2)}, u32[]{:S(2)}) collective-permute-start(f32[2,40,128]{2,1,0:T(8,128)S(1)} %get-tuple-element.7), channel_id=1, source_target_pairs={{0,1},{1,0},{2,3},{3,2},{4,5},{5,4},{6,7},{7,6},{8,9},{9,8},{10,11... | collective-permute-start | bytes 122888 | tf_op jit(solution)/shard_map/ppermute | solution.py:140
  10.1 0.9 %collective-permute-done = f32[2,40,128]{2,1,0:T(8,128)S(1)} collective-permute-done((f32[2,40,128]{2,1,0:T(8,128)S(1)}, f32[2,40,128]{2,1,0:T(8,128)S(1)}, u32[]{:S(2)}, u32[]{:S(2)}) %collective-permute-start) | collective-permute-done | bytes 40992 | tf_op jit(solution)/shard_map/ppermute | solution.py:140
  11.0 1.1 %collective-permute-start.3 = (f32[2,40,128]{2,1,0:T(8,128)S(1)}, f32[2,40,128]{2,1,0:T(8,128)S(1)}, u32[]{:S(2)}, u32[]{:S(2)}) collective-permute-start(f32[2,40,128]{2,1,0:T(8,128)S(1)} %pad_maximum_fusion), channel_id=1, source_target_pairs={{0,6},{1,7},{2,4},{3,5},{4,2},{5,3},{6,0},{7,1},{8,14},{9,15},{10,... | collective-permute-start | bytes 122888 | tf_op jit(solution)/shard_map/ppermute | solution.py:140
  12.1 0.4 collective-permute-start.2
  12.4 1.9 %collective-permute-start.1 = (f32[2,40,128]{2,1,0:T(8,128)S(1)}, f32[2,40,128]{2,1,0:T(8,128)S(1)}, u32[]{:S(2)}, u32[]{:S(2)}) collective-permute-start(f32[2,40,128]{2,1,0:T(8,128)S(1)} %pad_maximum_fusion), channel_id=1, source_target_pairs={{0,2},{1,3},{2,0},{3,1},{4,6},{5,7},{6,4},{7,5},{8,10},{9,11},{10,... | collective-permute-start | bytes 122888 | tf_op jit(solution)/shard_map/ppermute | solution.py:140
  14.3 0.8 %collective-permute-done.3 = f32[2,40,128]{2,1,0:T(8,128)S(1)} collective-permute-done((f32[2,40,128]{2,1,0:T(8,128)S(1)}, f32[2,40,128]{2,1,0:T(8,128)S(1)}, u32[]{:S(2)}, u32[]{:S(2)}) %collective-permute-start.3) | collective-permute-done | bytes 40992 | tf_op jit(solution)/shard_map/ppermute | solution.py:140
  15.1 1.3 %collective-permute-done.2 = f32[2,40,128]{2,1,0:T(8,128)S(1)} collective-permute-done((f32[2,40,128]{2,1,0:T(8,128)S(1)}, f32[2,40,128]{2,1,0:T(8,128)S(1)}, u32[]{:S(2)}, u32[]{:S(2)}) %collective-permute-start.2) | collective-permute-done | bytes 40992 | tf_op jit(solution)/shard_map/ppermute | solution.py:140
  16.4 0.0 collective-permute-done.1
  16.5 2.6 %collective-permute-start.6 = (f32[2,40,128]{2,1,0:T(8,128)S(1)}, f32[2,40,128]{2,1,0:T(8,128)S(1)}, u32[]{:S(2)}, u32[]{:S(2)}) collective-permute-start(f32[2,40,128]{2,1,0:T(8,128)S(1)} %pad_maximum_fusion.1), channel_id=1, source_target_pairs={{0,24},{1,25},{2,26},{3,27},{4,28},{5,29},{6,30},{7,31},{8,16},{9,... | collective-permute-start | bytes 122888 | tf_op jit(solution)/shard_map/ppermute | solution.py:140
  19.0 0.5 collective-permute-start.5
  19.6 0.2 collective-permute-start.4
  19.8 0.8 %collective-permute-done.6 = f32[2,40,128]{2,1,0:T(8,128)S(1)} collective-permute-done((f32[2,40,128]{2,1,0:T(8,128)S(1)}, f32[2,40,128]{2,1,0:T(8,128)S(1)}, u32[]{:S(2)}, u32[]{:S(2)}) %collective-permute-start.6) | collective-permute-done | bytes 40992 | tf_op jit(solution)/shard_map/ppermute | solution.py:140
  20.6 2.8 %collective-permute-done.5 = f32[2,40,128]{2,1,0:T(8,128)S(1)} collective-permute-done((f32[2,40,128]{2,1,0:T(8,128)S(1)}, f32[2,40,128]{2,1,0:T(8,128)S(1)}, u32[]{:S(2)}, u32[]{:S(2)}) %collective-permute-start.5) | collective-permute-done | bytes 40992 | tf_op jit(solution)/shard_map/ppermute | solution.py:140
  23.4 0.0 collective-permute-done.4
  23.4 1.7 %collective-permute-start.7 = (f32[2,40,128]{2,1,0:T(8,128)S(1)}, f32[2,40,128]{2,1,0:T(8,128)S(1)}, u32[]{:S(2)}, u32[]{:S(2)}) collective-permute-start(f32[2,40,128]{2,1,0:T(8,128)S(1)} %pad_maximum_fusion.2), channel_id=1, source_target_pairs={{0,32},{1,33},{2,34},{3,35},{4,36},{5,37},{6,38},{7,39},{8,40},{9,... | collective-permute-start | bytes 122888 | tf_op jit(solution)/shard_map/ppermute | solution.py:140
  25.2 1.4 %collective-permute-done.7 = f32[2,40,128]{2,1,0:T(8,128)S(1)} collective-permute-done((f32[2,40,128]{2,1,0:T(8,128)S(1)}, f32[2,40,128]{2,1,0:T(8,128)S(1)}, u32[]{:S(2)}, u32[]{:S(2)}) %collective-permute-start.7) | collective-permute-done | bytes 40992 | tf_op jit(solution)/shard_map/ppermute | solution.py:140
  26.6 5.9 %collective-permute-start.10 = (f32[2,40,128]{2,1,0:T(8,128)S(1)}, f32[2,40,128]{2,1,0:T(8,128)S(1)}, u32[]{:S(2)}, u32[]{:S(2)}) collective-permute-start(f32[2,40,128]{2,1,0:T(8,128)S(1)} %pad_maximum_fusion.3), channel_id=1, source_target_pairs={{0,192},{1,193},{2,194},{3,195},{4,196},{5,197},{6,198},{7,199},{8... | collective-permute-start | bytes 122888 | tf_op jit(solution)/shard_map/ppermute | solution.py:140
  32.5 0.0 collective-permute-start.9
  32.5 2.8 %collective-permute-start.8 = (f32[2,40,128]{2,1,0:T(8,128)S(1)}, f32[2,40,128]{2,1,0:T(8,128)S(1)}, u32[]{:S(2)}, u32[]{:S(2)}) collective-permute-start(f32[2,40,128]{2,1,0:T(8,128)S(1)} %pad_maximum_fusion.3), channel_id=1, source_target_pairs={{0,160},{1,161},{2,162},{3,163},{4,164},{5,165},{6,166},{7,167},{8... | collective-permute-start | bytes 122888 | tf_op jit(solution)/shard_map/ppermute | solution.py:140
  35.3 0.0 collective-permute-done.10
  35.3 2.2 %collective-permute-done.9 = f32[2,40,128]{2,1,0:T(8,128)S(1)} collective-permute-done((f32[2,40,128]{2,1,0:T(8,128)S(1)}, f32[2,40,128]{2,1,0:T(8,128)S(1)}, u32[]{:S(2)}, u32[]{:S(2)}) %collective-permute-start.9) | collective-permute-done | bytes 40992 | tf_op jit(solution)/shard_map/ppermute | solution.py:140
  37.5 0.9 %collective-permute-done.8 = f32[2,40,128]{2,1,0:T(8,128)S(1)} collective-permute-done((f32[2,40,128]{2,1,0:T(8,128)S(1)}, f32[2,40,128]{2,1,0:T(8,128)S(1)}, u32[]{:S(2)}, u32[]{:S(2)}) %collective-permute-start.8) | collective-permute-done | bytes 40992 | tf_op jit(solution)/shard_map/ppermute | solution.py:140
  38.4 6.2 %collective-permute-start.11 = (f32[2,40,128]{2,1,0:T(8,128)S(1)}, f32[2,40,128]{2,1,0:T(8,128)S(1)}, u32[]{:S(2)}, u32[]{:S(2)}) collective-permute-start(f32[2,40,128]{2,1,0:T(8,128)S(1)} %pad_maximum_fusion.4.mine_ref), channel_id=1, source_target_pairs={{0,1},{1,0},{2,3},{3,2},{4,5},{5,4},{6,7},{7,6},{8,9},{9,8},{10,11... | collective-permute-start | bytes 122888 | tf_op jit(solution)/shard_map/ppermute | solution.py:140
  44.7 0.9 %collective-permute-done.11.other_ref = f32[2,40,128]{2,1,0:T(8,128)S(1)} collective-permute-done((f32[2,40,128]{2,1,0:T(8,128)S(1)}, f32[2,40,128]{2,1,0:T(8,128)S(1)}, u32[]{:S(2)}, u32[]{:S(2)}) %collective-permute-start.11) | collective-permute-done | bytes 40992 | tf_op jit(solution)/shard_map/ppermute | solution.py:140
  45.5 0.0 copy-done.2
  45.5 0.0 copy-done.1
  45.5 0.0 copy-done
  45.5 14.1 %finish.1 = (f32[16,16384]{1,0:T(8,128)}, f32[128,128]{1,0:T(8,128)}, f32[128,128]{1,0:T(8,128)}) custom-call(f32[2,40,128]{2,1,0:T(8,128)S(1)} %pad_maximum_fusion.4.mine_ref, f32[2,40,128]{2,1,0:T(8,128)S(1)} %collective-permute-done.11.other_ref, f32[128,128]{1,0:T(8,128)S(1)} %copy-done, s32[16]{0:T(128)S(1)} %copy-done.1, f32[16]{0:T(128)S(1)} %copy-done.2, ...), custom_call_target="tpu_custom_call" | custom-call | tf_op jit(solution)/shard_map/finish/pallas_call | solution.py:367
  (10 shorter events, 0.1 us)
Async XLA Ops:
  0.6 44.9 %copy-start.2 = (f32[16]{0:T(128)S(1)}, f32[16]{0:T(128)}, u32[]{:S(2)}) copy-start(f32[16]{0:T(128)} %coef_ref.1) | copy-start | bytes 196
  0.6 44.9 %copy-start.1 = (s32[16]{0:T(128)S(1)}, s32[16]{0:T(128)}, u32[]{:S(2)}) copy-start(s32[16]{0:T(128)} %index_ref.1) | copy-start | bytes 196
  0.7 44.9 %copy-start = (f32[128,128]{1,0:T(8,128)S(1)}, f32[128,128]{1,0:T(8,128)}, u32[]{:S(2)}) copy-start(f32[128,128]{1,0:T(8,128)} %table_ref.1) | copy-start | bytes 196612
  6.8 4.2 %collective-permute-start = (f32[2,40,128]{2,1,0:T(8,128)S(1)}, f32[2,40,128]{2,1,0:T(8,128)S(1)}, u32[]{:S(2)}, u32[]{:S(2)}) collective-permute-start(f32[2,40,128]{2,1,0:T(8,128)S(1)} %get-tuple-element.7), channel_id=1, source_target_pairs={{0,1},{1,0},{2,3},{3,2},{4,5},{5,4},{6,7},{7,6},{8,9},{9,8},{10,11... | collective-permute-start | bytes 122888 | tf_op jit(solution)/shard_map/ppermute | solution.py:140
  11.0 4.2 %collective-permute-start.3 = (f32[2,40,128]{2,1,0:T(8,128)S(1)}, f32[2,40,128]{2,1,0:T(8,128)S(1)}, u32[]{:S(2)}, u32[]{:S(2)}) collective-permute-start(f32[2,40,128]{2,1,0:T(8,128)S(1)} %pad_maximum_fusion), channel_id=1, source_target_pairs={{0,6},{1,7},{2,4},{3,5},{4,2},{5,3},{6,0},{7,1},{8,14},{9,15},{10,... | collective-permute-start | bytes 122888 | tf_op jit(solution)/shard_map/ppermute | solution.py:140
  12.1 4.4 %collective-permute-start.2 = (f32[2,40,128]{2,1,0:T(8,128)S(1)}, f32[2,40,128]{2,1,0:T(8,128)S(1)}, u32[]{:S(2)}, u32[]{:S(2)}) collective-permute-start(f32[2,40,128]{2,1,0:T(8,128)S(1)} %pad_maximum_fusion), channel_id=1, source_target_pairs={{0,4},{1,5},{2,6},{3,7},{4,0},{5,1},{6,2},{7,3},{8,12},{9,13},{10,... | collective-permute-start | bytes 122888 | tf_op jit(solution)/shard_map/ppermute | solution.py:140
  12.4 4.0 %collective-permute-start.1 = (f32[2,40,128]{2,1,0:T(8,128)S(1)}, f32[2,40,128]{2,1,0:T(8,128)S(1)}, u32[]{:S(2)}, u32[]{:S(2)}) collective-permute-start(f32[2,40,128]{2,1,0:T(8,128)S(1)} %pad_maximum_fusion), channel_id=1, source_target_pairs={{0,2},{1,3},{2,0},{3,1},{4,6},{5,7},{6,4},{7,5},{8,10},{9,11},{10,... | collective-permute-start | bytes 122888 | tf_op jit(solution)/shard_map/ppermute | solution.py:140
  16.5 4.2 %collective-permute-start.6 = (f32[2,40,128]{2,1,0:T(8,128)S(1)}, f32[2,40,128]{2,1,0:T(8,128)S(1)}, u32[]{:S(2)}, u32[]{:S(2)}) collective-permute-start(f32[2,40,128]{2,1,0:T(8,128)S(1)} %pad_maximum_fusion.1), channel_id=1, source_target_pairs={{0,24},{1,25},{2,26},{3,27},{4,28},{5,29},{6,30},{7,31},{8,16},{9,... | collective-permute-start | bytes 122888 | tf_op jit(solution)/shard_map/ppermute | solution.py:140
  19.0 4.4 %collective-permute-start.5 = (f32[2,40,128]{2,1,0:T(8,128)S(1)}, f32[2,40,128]{2,1,0:T(8,128)S(1)}, u32[]{:S(2)}, u32[]{:S(2)}) collective-permute-start(f32[2,40,128]{2,1,0:T(8,128)S(1)} %pad_maximum_fusion.1), channel_id=1, source_target_pairs={{0,16},{1,17},{2,18},{3,19},{4,20},{5,21},{6,22},{7,23},{8,24},{9,... | collective-permute-start | bytes 122888 | tf_op jit(solution)/shard_map/ppermute | solution.py:140
  19.6 3.8 %collective-permute-start.4 = (f32[2,40,128]{2,1,0:T(8,128)S(1)}, f32[2,40,128]{2,1,0:T(8,128)S(1)}, u32[]{:S(2)}, u32[]{:S(2)}) collective-permute-start(f32[2,40,128]{2,1,0:T(8,128)S(1)} %pad_maximum_fusion.1), channel_id=1, source_target_pairs={{0,8},{1,9},{2,10},{3,11},{4,12},{5,13},{6,14},{7,15},{8,0},{9,1},... | collective-permute-start | bytes 122888 | tf_op jit(solution)/shard_map/ppermute | solution.py:140
  23.4 3.1 %collective-permute-start.7 = (f32[2,40,128]{2,1,0:T(8,128)S(1)}, f32[2,40,128]{2,1,0:T(8,128)S(1)}, u32[]{:S(2)}, u32[]{:S(2)}) collective-permute-start(f32[2,40,128]{2,1,0:T(8,128)S(1)} %pad_maximum_fusion.2), channel_id=1, source_target_pairs={{0,32},{1,33},{2,34},{3,35},{4,36},{5,37},{6,38},{7,39},{8,40},{9,... | collective-permute-start | bytes 122888 | tf_op jit(solution)/shard_map/ppermute | solution.py:140
  26.6 8.7 %collective-permute-start.10 = (f32[2,40,128]{2,1,0:T(8,128)S(1)}, f32[2,40,128]{2,1,0:T(8,128)S(1)}, u32[]{:S(2)}, u32[]{:S(2)}) collective-permute-start(f32[2,40,128]{2,1,0:T(8,128)S(1)} %pad_maximum_fusion.3), channel_id=1, source_target_pairs={{0,192},{1,193},{2,194},{3,195},{4,196},{5,197},{6,198},{7,199},{8... | collective-permute-start | bytes 122888 | tf_op jit(solution)/shard_map/ppermute | solution.py:140
  32.5 5.0 %collective-permute-start.9 = (f32[2,40,128]{2,1,0:T(8,128)S(1)}, f32[2,40,128]{2,1,0:T(8,128)S(1)}, u32[]{:S(2)}, u32[]{:S(2)}) collective-permute-start(f32[2,40,128]{2,1,0:T(8,128)S(1)} %pad_maximum_fusion.3), channel_id=1, source_target_pairs={{0,64},{1,65},{2,66},{3,67},{4,68},{5,69},{6,70},{7,71},{8,72},{9,... | collective-permute-start | bytes 122888 | tf_op jit(solution)/shard_map/ppermute | solution.py:140
  32.5 5.9 %collective-permute-start.8 = (f32[2,40,128]{2,1,0:T(8,128)S(1)}, f32[2,40,128]{2,1,0:T(8,128)S(1)}, u32[]{:S(2)}, u32[]{:S(2)}) collective-permute-start(f32[2,40,128]{2,1,0:T(8,128)S(1)} %pad_maximum_fusion.3), channel_id=1, source_target_pairs={{0,160},{1,161},{2,162},{3,163},{4,164},{5,165},{6,166},{7,167},{8... | collective-permute-start | bytes 122888 | tf_op jit(solution)/shard_map/ppermute | solution.py:140
  38.4 7.1 %collective-permute-start.11 = (f32[2,40,128]{2,1,0:T(8,128)S(1)}, f32[2,40,128]{2,1,0:T(8,128)S(1)}, u32[]{:S(2)}, u32[]{:S(2)}) collective-permute-start(f32[2,40,128]{2,1,0:T(8,128)S(1)} %pad_maximum_fusion.4.mine_ref), channel_id=1, source_target_pairs={{0,1},{1,0},{2,3},{3,2},{4,5},{5,4},{6,7},{7,6},{8,9},{9,8},{10,11... | collective-permute-start | bytes 122888 | tf_op jit(solution)/shard_map/ppermute | solution.py:140

commit v2 on v1

--- a/solution.py
+++ b/solution.py
@@ -39,7 +39,20 @@
     return lax.broadcasted_iota(jnp.int32, shape, axis)
 
 
-def gram_body(chunk, part, panel_ref, kept_ref, sent_ref, x_ref, high_ref, low_ref, cross_ref, mid_ref, last_ref, sems):
+def gram_body(
+    chunk,
+    part,
+    panel_ref,
+    kept_ref,
+    sent_ref,
+    x_ref,
+    high_ref,
+    low_ref,
+    cross_ref,
+    mid_ref,
+    last_ref,
+    sems,
+):
     count = panel_ref.shape[1] // chunk
     for index in range(count):
         fetch(panel_ref, x_ref, sems, chunk, index).start()
@@ -122,7 +135,8 @@
     return pl.pallas_call(
         functools.partial(gram_body, chunk, part),
         in_specs=[pl.BlockSpec(memory_space=pl.ANY)],
-        out_shape=[pltpu.VMEM((2, HALF, 128), F32)] * 2 + [pltpu.VMEM((snaps, columns), F32)],
+        out_shape=[pltpu.VMEM((2, HALF, 128), F32)] * 2
+        + [pltpu.VMEM((snaps, columns), F32)],
         out_specs=[pl.BlockSpec(memory_space=pltpu.VMEM)] * 3,
         scratch_shapes=[square] * 5
         + [pltpu.SemaphoreType.DMA((columns // chunk,))],
@@ -146,16 +160,12 @@
 
 def sum_pairs(kept, sent, size):
     half = pair_add(kept, exchange(sent, flips(size, 1)))
-    for step in (2, 8):
+    for step in (2, 8, 32):
         first = exchange(half, flips(size, step))
         second = exchange(half, flips(size, 2 * step))
         third = exchange(half, flips(size, 3 * step))
         half = pair_add(pair_add(half, first), pair_add(second, third))
-    half = pair_add(half, exchange(half, flips(size, 32)))
-    before = exchange(half, [(i, (i + 64) % size) for i in range(size)])
-    after = exchange(half, [(i, (i - 64) % size) for i in range(size)])
-    across = exchange(half, flips(size, 160))
-    half = pair_add(pair_add(half, across), pair_add(before, after))
+    half = pair_add(half, exchange(half, flips(size, 224)))
     return half, exchange(half, flips(size, 1))
 
 
@@ -255,9 +265,16 @@
     factor_ref,
     y_ref,
     shift_ref,
+    small_ref,
+    small_sems,
     out_sems,
 ):
     columns = x_ref.shape[1]
+    own = iota((16, 16), 0) == iota((16, 16), 1)
+    index = jnp.sum(jnp.where(own, index_ref[...], 0), axis=1, keepdims=True)
+    coef = jnp.sum(jnp.where(own, coef_ref[...], 0.0), axis=1, keepdims=True)
+    onehot = (iota((16, 128), 1) == index).astype(F32)
+    chosen = dot(onehot, table_ref[...], NT, HIGH) * (coef * root)
     even = even_core()
     mine, other = mine_ref[...], other_ref[...]
     packed = jnp.concatenate([jnp.where(even, mine, other), jnp.where(even, other, mine)], axis=1)
@@ -280,7 +297,9 @@
     last_low = last_low * last_scale
 
     upper, lower_inverse = factor(gram_high)
-    factor_ref[...] = upper * (unscale * (1.0 / root))
+    small_ref[0] = upper * (unscale * (1.0 / root))
+    factor_out = pltpu.make_async_copy(small_ref.at[0], factor_ref, small_sems.at[0])
+    factor_out.start()
 
     norms = jnp.sum(lower_inverse * lower_inverse, axis=1, keepdims=True)
     row_scale, _ = power_scale(jnp.broadcast_to(norms, (128, 128)))
@@ -316,16 +335,10 @@
     z = shift_ref[1:129]
     following = jnp.where(iota((1, 128), 1) == 127, last_unscale, pltpu.roll(unscale, 127, 1))
     h = dot(whole * (scale * following), z, NN, HIGH)
-    operator_ref[...] = dot(second, h, NT, HIGH)
-
-    rows = iota((16, 128), 0)
-    index, coef = jnp.zeros((16, 128), jnp.int32), jnp.zeros((16, 128), F32)
-    for mode in range(16):
-        index = jnp.where(rows == mode, index_ref[mode], index)
-        coef = jnp.where(rows == mode, coef_ref[mode], coef)
-    onehot = (iota((16, 128), 1) == index).astype(F32)
-    chosen = dot(onehot, table_ref[...], NT, HIGH)
-    comb = dot(chosen, whole, NN, HIGH) * scale * (coef * root)
+    small_ref[1] = dot(second, h, NT, HIGH)
+    operator_out = pltpu.make_async_copy(small_ref.at[1], operator_ref, small_sems.at[1])
+    operator_out.start()
+    comb = dot(chosen, whole, NN, HIGH) * scale
 
     shifted = jnp.where(iota(comb.shape, 1) == 0, 0.0, pltpu.roll(comb, 1, 1))
     c = split3(shifted)
@@ -355,19 +368,18 @@
     lax.fori_loop(0, columns // out_chunk, step, 0)
     for index in range(columns // out_chunk):
         send(index).wait()
-
-
-def finish(mine, other, table, index, coef, panel, total_rows, out_chunk=2048):
-    root = float(total_rows) ** 0.5
-    modes = index.shape[0]
-    columns = panel.shape[1]
+    factor_out.wait()
+    operator_out.wait()
+
+
+def finish(mine, other, table, index, coef, panel, root, out_chunk=4096):
+    modes, columns = index.shape[0], panel.shape[1]
     whole = pl.BlockSpec(memory_space=pltpu.VMEM)
     remote = pl.BlockSpec(memory_space=pl.ANY)
-    scalars = pl.BlockSpec(memory_space=pltpu.SMEM)
     return pl.pallas_call(
         functools.partial(finish_body, root, out_chunk),
-        in_specs=[whole] * 3 + [scalars] * 2 + [whole],
-        out_specs=[remote, whole, whole],
+        in_specs=[whole] * 6,
+        out_specs=[remote] * 3,
         out_shape=[
             jax.ShapeDtypeStruct((modes, columns), F32),
             jax.ShapeDtypeStruct((128, 128), F32),
@@ -376,17 +388,20 @@
         scratch_shapes=[
             pltpu.VMEM((modes, columns), F32),
             pltpu.VMEM((136, 128), F32),
+            pltpu.VMEM((2, 128, 128), F32),
+            pltpu.SemaphoreType.DMA((2,)),
             pltpu.SemaphoreType.DMA((columns // out_chunk,)),
         ],
         compiler_params=pltpu.CompilerParams(vmem_limit_bytes=LIMIT),
         name="finish",
-    )(mine, other, table, index, coef, panel)
+    )(mine, other, table, index.reshape(1, modes), coef.reshape(1, modes), panel)
 
 
 def local(size, panel, eig_table, mode_index, mode_coef):
+    root = float(panel.shape[1] * size) ** 0.5
     kept, sent, held = local_gram(panel)
     mine, other = sum_pairs(kept, sent, size)
-    return tuple(finish(mine, other, eig_table, mode_index, mode_coef, held, panel.shape[1] * size))
+    return tuple(finish(mine, other, eig_table, mode_index, mode_coef, held, root))
 
 
 def solution(mesh):

time: 59.9 us -> 55.5 us (0.927)
  starting transfers between devices: 26.7 us -> 23.4 us
  Pallas kernels: 20.2 us -> 18.6 us
    ppermute x12, starting transfers between devices: 26.7 us -> 23.4 us  [exchange(): return lax.ppermute(x, 'space', pairs)]
    pallas_call x1, Pallas kernels: 14.1 us -> 12.5 us  [finish(): pl.pallas_call(functools.partial(finish_body, root, out_chunk), in_specs=...]
where the time goes in v2:
time: 55.5 us
  starting transfers between devices  23.4 us (42%)
  Pallas kernels  18.6 us (34%)
  waiting for transfers between devices  12.4 us (22%)
  between operations  0.89 us (2%)
    ppermute x12, starting transfers between devices, exchange(): return lax.ppermute(x, 'space', pairs)  23.4 us
    pallas_call x1, Pallas kernels, finish(): pl.pallas_call(functools.partial(finish_body, root, out_chunk), in_specs=...  12.5 us
    ppermute x12, waiting for transfers between devices, exchange(): return lax.ppermute(x, 'space', pairs)  12.4 us
    pallas_call x1, Pallas kernels, local_gram(): pl.pallas_call(functools.partial(gram_body, chunk, part), in_specs=[pl.Bl...  6.09 us
  transfers between devices with their start and end apart: 12, of which 9 were waited for; matrix products, arithmetic and copies ran while one was open for 0% of the time, Pallas kernels for 0%

profile of v2, /device:TPU:1, one launch (start us, length us, event | category | flops | bytes accessed | tf_op | source)
XLA Modules:
  0.0 55.5 jit_solution(8373733090720100317)
XLA Ops:
  0.6 0.0 copy-start.2
  0.6 0.0 copy-start.1
  0.7 0.0 copy-start
  0.7 6.1 %gram.1 = (f32[2,40,128]{2,1,0:T(8,128)S(1)}, f32[2,40,128]{2,1,0:T(8,128)S(1)}, f32[129,16384]{1,0:T(8,128)S(1)}) custom-call(f32[129,16384]{1,0:T(8,128)} %panel_ref.1), custom_call_target="tpu_custom_call" | custom-call | tf_op jit(solution)/shard_map/gram/pallas_call | solution.py:135
  6.8 3.3 %collective-permute-start = (f32[2,40,128]{2,1,0:T(8,128)S(1)}, f32[2,40,128]{2,1,0:T(8,128)S(1)}, u32[]{:S(2)}, u32[]{:S(2)}) collective-permute-start(f32[2,40,128]{2,1,0:T(8,128)S(1)} %get-tuple-element.7), channel_id=1, source_target_pairs={{0,1},{1,0},{2,3},{3,2},{4,5},{5,4},{6,7},{7,6},{8,9},{9,8},{10,11... | collective-permute-start | bytes 122888 | tf_op jit(solution)/shard_map/ppermute | solution.py:154
  10.1 0.9 %collective-permute-done = f32[2,40,128]{2,1,0:T(8,128)S(1)} collective-permute-done((f32[2,40,128]{2,1,0:T(8,128)S(1)}, f32[2,40,128]{2,1,0:T(8,128)S(1)}, u32[]{:S(2)}, u32[]{:S(2)}) %collective-permute-start) | collective-permute-done | bytes 40992 | tf_op jit(solution)/shard_map/ppermute | solution.py:154
  11.0 1.1 %collective-permute-start.3 = (f32[2,40,128]{2,1,0:T(8,128)S(1)}, f32[2,40,128]{2,1,0:T(8,128)S(1)}, u32[]{:S(2)}, u32[]{:S(2)}) collective-permute-start(f32[2,40,128]{2,1,0:T(8,128)S(1)} %pad_maximum_fusion), channel_id=1, source_target_pairs={{0,6},{1,7},{2,4},{3,5},{4,2},{5,3},{6,0},{7,1},{8,14},{9,15},{10,... | collective-permute-start | bytes 122888 | tf_op jit(solution)/shard_map/ppermute | solution.py:154
  12.1 0.4 collective-permute-start.2
  12.4 1.9 %collective-permute-start.1 = (f32[2,40,128]{2,1,0:T(8,128)S(1)}, f32[2,40,128]{2,1,0:T(8,128)S(1)}, u32[]{:S(2)}, u32[]{:S(2)}) collective-permute-start(f32[2,40,128]{2,1,0:T(8,128)S(1)} %pad_maximum_fusion), channel_id=1, source_target_pairs={{0,2},{1,3},{2,0},{3,1},{4,6},{5,7},{6,4},{7,5},{8,10},{9,11},{10,... | collective-permute-start | bytes 122888 | tf_op jit(solution)/shard_map/ppermute | solution.py:154
  14.3 0.8 %collective-permute-done.3 = f32[2,40,128]{2,1,0:T(8,128)S(1)} collective-permute-done((f32[2,40,128]{2,1,0:T(8,128)S(1)}, f32[2,40,128]{2,1,0:T(8,128)S(1)}, u32[]{:S(2)}, u32[]{:S(2)}) %collective-permute-start.3) | collective-permute-done | bytes 40992 | tf_op jit(solution)/shard_map/ppermute | solution.py:154
  15.1 1.3 %collective-permute-done.2 = f32[2,40,128]{2,1,0:T(8,128)S(1)} collective-permute-done((f32[2,40,128]{2,1,0:T(8,128)S(1)}, f32[2,40,128]{2,1,0:T(8,128)S(1)}, u32[]{:S(2)}, u32[]{:S(2)}) %collective-permute-start.2) | collective-permute-done | bytes 40992 | tf_op jit(solution)/shard_map/ppermute | solution.py:154
  16.4 0.0 collective-permute-done.1
  16.5 2.6 %collective-permute-start.6 = (f32[2,40,128]{2,1,0:T(8,128)S(1)}, f32[2,40,128]{2,1,0:T(8,128)S(1)}, u32[]{:S(2)}, u32[]{:S(2)}) collective-permute-start(f32[2,40,128]{2,1,0:T(8,128)S(1)} %pad_maximum_fusion.1), channel_id=1, source_target_pairs={{0,24},{1,25},{2,26},{3,27},{4,28},{5,29},{6,30},{7,31},{8,16},{9,... | collective-permute-start | bytes 122888 | tf_op jit(solution)/shard_map/ppermute | solution.py:154
  19.0 0.5 collective-permute-start.5
  19.6 0.2 collective-permute-start.4
  19.8 0.8 %collective-permute-done.6 = f32[2,40,128]{2,1,0:T(8,128)S(1)} collective-permute-done((f32[2,40,128]{2,1,0:T(8,128)S(1)}, f32[2,40,128]{2,1,0:T(8,128)S(1)}, u32[]{:S(2)}, u32[]{:S(2)}) %collective-permute-start.6) | collective-permute-done | bytes 40992 | tf_op jit(solution)/shard_map/ppermute | solution.py:154
  20.6 2.8 %collective-permute-done.5 = f32[2,40,128]{2,1,0:T(8,128)S(1)} collective-permute-done((f32[2,40,128]{2,1,0:T(8,128)S(1)}, f32[2,40,128]{2,1,0:T(8,128)S(1)}, u32[]{:S(2)}, u32[]{:S(2)}) %collective-permute-start.5) | collective-permute-done | bytes 40992 | tf_op jit(solution)/shard_map/ppermute | solution.py:154
  23.4 0.0 collective-permute-done.4
  23.4 4.4 %collective-permute-start.9 = (f32[2,40,128]{2,1,0:T(8,128)S(1)}, f32[2,40,128]{2,1,0:T(8,128)S(1)}, u32[]{:S(2)}, u32[]{:S(2)}) collective-permute-start(f32[2,40,128]{2,1,0:T(8,128)S(1)} %pad_maximum_fusion.2), channel_id=1, source_target_pairs={{0,96},{1,97},{2,98},{3,99},{4,100},{5,101},{6,102},{7,103},{8,104... | collective-permute-start | bytes 122888 | tf_op jit(solution)/shard_map/ppermute | solution.py:154
  27.9 0.0 collective-permute-start.8
  27.9 0.4 collective-permute-start.7
  28.3 1.0 %collective-permute-done.9 = f32[2,40,128]{2,1,0:T(8,128)S(1)} collective-permute-done((f32[2,40,128]{2,1,0:T(8,128)S(1)}, f32[2,40,128]{2,1,0:T(8,128)S(1)}, u32[]{:S(2)}, u32[]{:S(2)}) %collective-permute-start.9) | collective-permute-done | bytes 40992 | tf_op jit(solution)/shard_map/ppermute | solution.py:154
  29.3 2.6 %collective-permute-done.8 = f32[2,40,128]{2,1,0:T(8,128)S(1)} collective-permute-done((f32[2,40,128]{2,1,0:T(8,128)S(1)}, f32[2,40,128]{2,1,0:T(8,128)S(1)}, u32[]{:S(2)}, u32[]{:S(2)}) %collective-permute-start.8) | collective-permute-done | bytes 40992 | tf_op jit(solution)/shard_map/ppermute | solution.py:154
  31.9 0.0 collective-permute-done.7
  31.9 2.9 %collective-permute-start.10 = (f32[2,40,128]{2,1,0:T(8,128)S(1)}, f32[2,40,128]{2,1,0:T(8,128)S(1)}, u32[]{:S(2)}, u32[]{:S(2)}) collective-permute-start(f32[2,40,128]{2,1,0:T(8,128)S(1)} %pad_maximum_fusion.3), channel_id=1, source_target_pairs={{0,224},{1,225},{2,226},{3,227},{4,228},{5,229},{6,230},{7,231},{8... | collective-permute-start | bytes 122888 | tf_op jit(solution)/shard_map/ppermute | solution.py:154
  34.8 1.4 %collective-permute-done.10 = f32[2,40,128]{2,1,0:T(8,128)S(1)} collective-permute-done((f32[2,40,128]{2,1,0:T(8,128)S(1)}, f32[2,40,128]{2,1,0:T(8,128)S(1)}, u32[]{:S(2)}, u32[]{:S(2)}) %collective-permute-start.10) | collective-permute-done | bytes 40992 | tf_op jit(solution)/shard_map/ppermute | solution.py:154
  36.2 5.7 %collective-permute-start.11 = (f32[2,40,128]{2,1,0:T(8,128)S(1)}, f32[2,40,128]{2,1,0:T(8,128)S(1)}, u32[]{:S(2)}, u32[]{:S(2)}) collective-permute-start(f32[2,40,128]{2,1,0:T(8,128)S(1)} %pad_maximum_fusion.4.mine_ref), channel_id=1, source_target_pairs={{0,1},{1,0},{2,3},{3,2},{4,5},{5,4},{6,7},{7,6},{8,9},{9,8},{10,11... | collective-permute-start | bytes 122888 | tf_op jit(solution)/shard_map/ppermute | solution.py:154
  41.9 0.9 %collective-permute-done.11.other_ref = f32[2,40,128]{2,1,0:T(8,128)S(1)} collective-permute-done((f32[2,40,128]{2,1,0:T(8,128)S(1)}, f32[2,40,128]{2,1,0:T(8,128)S(1)}, u32[]{:S(2)}, u32[]{:S(2)}) %collective-permute-start.11) | collective-permute-done | bytes 40992 | tf_op jit(solution)/shard_map/ppermute | solution.py:154
  42.8 0.0 copy-done.2
  42.8 0.0 copy-done.1
  42.8 0.0 copy-done
  42.8 12.5 %finish.1 = (f32[16,16384]{1,0:T(8,128)}, f32[128,128]{1,0:T(8,128)}, f32[128,128]{1,0:T(8,128)}) custom-call(f32[2,40,128]{2,1,0:T(8,128)S(1)} %pad_maximum_fusion.4.mine_ref, f32[2,40,128]{2,1,0:T(8,128)S(1)} %collective-permute-done.11.other_ref, f32[128,128]{1,0:T(8,128)S(1)} %copy-done, s32[1,16]{1,0:T(1,128)S(1)} %bitcast.2, f32[1,16]{1,0:T(1,128)S(1)} %bitcast.3, ...), custom_call_target="tpu_custom_call" | custom-call | tf_op jit(solution)/shard_map/finish/pallas_call | solution.py:379
  (10 shorter events, 0.1 us)
Async XLA Ops:
  0.6 42.2 %copy-start.2 = (f32[16]{0:T(128)S(1)}, f32[16]{0:T(128)}, u32[]{:S(2)}) copy-start(f32[16]{0:T(128)} %param.7) | copy-start | bytes 196
  0.6 42.2 %copy-start.1 = (s32[16]{0:T(128)S(1)}, s32[16]{0:T(128)}, u32[]{:S(2)}) copy-start(s32[16]{0:T(128)} %param.6) | copy-start | bytes 196
  0.7 42.1 %copy-start = (f32[128,128]{1,0:T(8,128)S(1)}, f32[128,128]{1,0:T(8,128)}, u32[]{:S(2)}) copy-start(f32[128,128]{1,0:T(8,128)} %table_ref.1) | copy-start | bytes 196612
  6.8 4.2 %collective-permute-start = (f32[2,40,128]{2,1,0:T(8,128)S(1)}, f32[2,40,128]{2,1,0:T(8,128)S(1)}, u32[]{:S(2)}, u32[]{:S(2)}) collective-permute-start(f32[2,40,128]{2,1,0:T(8,128)S(1)} %get-tuple-element.7), channel_id=1, source_target_pairs={{0,1},{1,0},{2,3},{3,2},{4,5},{5,4},{6,7},{7,6},{8,9},{9,8},{10,11... | collective-permute-start | bytes 122888 | tf_op jit(solution)/shard_map/ppermute | solution.py:154
  11.0 4.2 %collective-permute-start.3 = (f32[2,40,128]{2,1,0:T(8,128)S(1)}, f32[2,40,128]{2,1,0:T(8,128)S(1)}, u32[]{:S(2)}, u32[]{:S(2)}) collective-permute-start(f32[2,40,128]{2,1,0:T(8,128)S(1)} %pad_maximum_fusion), channel_id=1, source_target_pairs={{0,6},{1,7},{2,4},{3,5},{4,2},{5,3},{6,0},{7,1},{8,14},{9,15},{10,... | collective-permute-start | bytes 122888 | tf_op jit(solution)/shard_map/ppermute | solution.py:154
  12.1 4.4 %collective-permute-start.2 = (f32[2,40,128]{2,1,0:T(8,128)S(1)}, f32[2,40,128]{2,1,0:T(8,128)S(1)}, u32[]{:S(2)}, u32[]{:S(2)}) collective-permute-start(f32[2,40,128]{2,1,0:T(8,128)S(1)} %pad_maximum_fusion), channel_id=1, source_target_pairs={{0,4},{1,5},{2,6},{3,7},{4,0},{5,1},{6,2},{7,3},{8,12},{9,13},{10,... | collective-permute-start | bytes 122888 | tf_op jit(solution)/shard_map/ppermute | solution.py:154
  12.4 4.0 %collective-permute-start.1 = (f32[2,40,128]{2,1,0:T(8,128)S(1)}, f32[2,40,128]{2,1,0:T(8,128)S(1)}, u32[]{:S(2)}, u32[]{:S(2)}) collective-permute-start(f32[2,40,128]{2,1,0:T(8,128)S(1)} %pad_maximum_fusion), channel_id=1, source_target_pairs={{0,2},{1,3},{2,0},{3,1},{4,6},{5,7},{6,4},{7,5},{8,10},{9,11},{10,... | collective-permute-start | bytes 122888 | tf_op jit(solution)/shard_map/ppermute | solution.py:154
  16.5 4.2 %collective-permute-start.6 = (f32[2,40,128]{2,1,0:T(8,128)S(1)}, f32[2,40,128]{2,1,0:T(8,128)S(1)}, u32[]{:S(2)}, u32[]{:S(2)}) collective-permute-start(f32[2,40,128]{2,1,0:T(8,128)S(1)} %pad_maximum_fusion.1), channel_id=1, source_target_pairs={{0,24},{1,25},{2,26},{3,27},{4,28},{5,29},{6,30},{7,31},{8,16},{9,... | collective-permute-start | bytes 122888 | tf_op jit(solution)/shard_map/ppermute | solution.py:154
  19.0 4.4 %collective-permute-start.5 = (f32[2,40,128]{2,1,0:T(8,128)S(1)}, f32[2,40,128]{2,1,0:T(8,128)S(1)}, u32[]{:S(2)}, u32[]{:S(2)}) collective-permute-start(f32[2,40,128]{2,1,0:T(8,128)S(1)} %pad_maximum_fusion.1), channel_id=1, source_target_pairs={{0,16},{1,17},{2,18},{3,19},{4,20},{5,21},{6,22},{7,23},{8,24},{9,... | collective-permute-start | bytes 122888 | tf_op jit(solution)/shard_map/ppermute | solution.py:154
  19.6 3.8 %collective-permute-start.4 = (f32[2,40,128]{2,1,0:T(8,128)S(1)}, f32[2,40,128]{2,1,0:T(8,128)S(1)}, u32[]{:S(2)}, u32[]{:S(2)}) collective-permute-start(f32[2,40,128]{2,1,0:T(8,128)S(1)} %pad_maximum_fusion.1), channel_id=1, source_target_pairs={{0,8},{1,9},{2,10},{3,11},{4,12},{5,13},{6,14},{7,15},{8,0},{9,1},... | collective-permute-start | bytes 122888 | tf_op jit(solution)/shard_map/ppermute | solution.py:154
  23.4 5.8 %collective-permute-start.9 = (f32[2,40,128]{2,1,0:T(8,128)S(1)}, f32[2,40,128]{2,1,0:T(8,128)S(1)}, u32[]{:S(2)}, u32[]{:S(2)}) collective-permute-start(f32[2,40,128]{2,1,0:T(8,128)S(1)} %pad_maximum_fusion.2), channel_id=1, source_target_pairs={{0,96},{1,97},{2,98},{3,99},{4,100},{5,101},{6,102},{7,103},{8,104... | collective-permute-start | bytes 122888 | tf_op jit(solution)/shard_map/ppermute | solution.py:154
  27.9 4.0 %collective-permute-start.8 = (f32[2,40,128]{2,1,0:T(8,128)S(1)}, f32[2,40,128]{2,1,0:T(8,128)S(1)}, u32[]{:S(2)}, u32[]{:S(2)}) collective-permute-start(f32[2,40,128]{2,1,0:T(8,128)S(1)} %pad_maximum_fusion.2), channel_id=1, source_target_pairs={{0,64},{1,65},{2,66},{3,67},{4,68},{5,69},{6,70},{7,71},{8,72},{9,... | collective-permute-start | bytes 122888 | tf_op jit(solution)/shard_map/ppermute | solution.py:154
  27.9 4.0 %collective-permute-start.7 = (f32[2,40,128]{2,1,0:T(8,128)S(1)}, f32[2,40,128]{2,1,0:T(8,128)S(1)}, u32[]{:S(2)}, u32[]{:S(2)}) collective-permute-start(f32[2,40,128]{2,1,0:T(8,128)S(1)} %pad_maximum_fusion.2), channel_id=1, source_target_pairs={{0,32},{1,33},{2,34},{3,35},{4,36},{5,37},{6,38},{7,39},{8,40},{9,... | collective-permute-start | bytes 122888 | tf_op jit(solution)/shard_map/ppermute | solution.py:154
  31.9 4.3 %collective-permute-start.10 = (f32[2,40,128]{2,1,0:T(8,128)S(1)}, f32[2,40,128]{2,1,0:T(8,128)S(1)}, u32[]{:S(2)}, u32[]{:S(2)}) collective-permute-start(f32[2,40,128]{2,1,0:T(8,128)S(1)} %pad_maximum_fusion.3), channel_id=1, source_target_pairs={{0,224},{1,225},{2,226},{3,227},{4,228},{5,229},{6,230},{7,231},{8... | collective-permute-start | bytes 122888 | tf_op jit(solution)/shard_map/ppermute | solution.py:154
  36.2 6.6 %collective-permute-start.11 = (f32[2,40,128]{2,1,0:T(8,128)S(1)}, f32[2,40,128]{2,1,0:T(8,128)S(1)}, u32[]{:S(2)}, u32[]{:S(2)}) collective-permute-start(f32[2,40,128]{2,1,0:T(8,128)S(1)} %pad_maximum_fusion.4.mine_ref), channel_id=1, source_target_pairs={{0,1},{1,0},{2,3},{3,2},{4,5},{5,4},{6,7},{7,6},{8,9},{9,8},{10,11... | collective-permute-start | bytes 122888 | tf_op jit(solution)/shard_map/ppermute | solution.py:154

commit v3 on v2

--- a/solution.py
+++ b/solution.py
@@ -208,31 +208,51 @@
     return two_sum(total, rest)
 
 
-def factor(matrix, size=16):
+def factor(matrix, size=32):
     count = 128 // size
     work = [matrix[size * i : size * i + size] for i in range(count)]
     lanes, rows = iota((size, 128), 1), iota((size, 128), 0)
+    tile_rows = iota((8, 128), 0)
     extra = [jnp.where(lanes == rows + size * i, 1.0, 0.0).astype(F32) for i in range(count)]
+    tiles = size // 8
+
+    def spread(row):
+        return jnp.broadcast_to(row, (8, 128))
+
     upper, inverse = [], []
     for block in range(count):
         at = size * block
-        wide, carried = work[block], extra[block]
-        columns = [jnp.broadcast_to(wide[:, at + k : at + k + 1], (size, 128)) for k in range(size)]
-        pivots = jnp.ones((size, 128), F32)
+        wide = [work[block][8 * t : 8 * t + 8] for t in range(tiles)]
+        carried = [extra[block][8 * t : 8 * t + 8] for t in range(tiles)]
+        columns = [
+            [None if t < k // 8 else spread(wide[t][:, at + k : at + k + 1]) for t in range(tiles)] for k in range(size)
+        ]
+        pivots = [jnp.ones((8, 128), F32) for _ in range(tiles)]
         for j in range(size):
-            pivot = columns[j][j : j + 1]
-            pivots = jnp.where(rows == j, jnp.broadcast_to(pivot, (size, 128)), pivots)
+            own, row = j // 8, j % 8
+            pivot = columns[j][own][row : row + 1]
+            pivots[own] = jnp.where(tile_rows == row, spread(pivot), pivots[own])
             if j == size - 1:
                 break
-            ratio = jnp.where(rows > j, columns[j] * jnp.broadcast_to(1.0 / pivot, (size, 128)), 0.0)
+            factor_row = spread(1.0 / pivot)
+            wide_row, carried_row = spread(wide[own][row : row + 1]), spread(carried[own][row : row + 1])
+            ratio = [None] * tiles
+            for t in range(own, tiles):
+                ratio[t] = columns[j][t] * factor_row
+                if t == own:
+                    ratio[t] = jnp.where(tile_rows > row, ratio[t], 0.0)
             for k in range(j + 1, size):
-                columns[k] = columns[k] - ratio * jnp.broadcast_to(columns[k][j : j + 1], (size, 128))
-            wide = wide - ratio * jnp.broadcast_to(wide[j : j + 1], (size, 128))
-            carried = carried - ratio * jnp.broadcast_to(carried[j : j + 1], (size, 128))
+                entry = spread(columns[j][k // 8][k % 8 : k % 8 + 1])
+                for t in range(k // 8, tiles):
+                    columns[k][t] = columns[k][t] - ratio[t] * entry
+            for t in range(own, tiles):
+                wide[t] = wide[t] - ratio[t] * wide_row
+                carried[t] = carried[t] - ratio[t] * carried_row
+        pivots = jnp.concatenate(pivots, axis=0)
         root = lax.rsqrt(pivots)
         root = root * (1.5 - 0.5 * pivots * root * root)
-        wide = jnp.where(lanes >= rows + at, wide * root, 0.0)
-        carried = carried * root
+        wide = jnp.where(lanes >= rows + at, jnp.concatenate(wide, axis=0) * root, 0.0)
+        carried = jnp.concatenate(carried, axis=0) * root
         upper.append(wide)
         inverse.append(carried)
         if block < count - 1:

time: 55.5 us -> 54.6 us (0.984)
  Pallas kernels: 18.6 us -> 17.6 us
    pallas_call x1, Pallas kernels: 12.5 us -> 11.5 us  [finish(): pl.pallas_call(functools.partial(finish_body, root, out_chunk), in_specs=...]
where the time goes in v3:
time: 54.6 us; the launch traced here: 54.5 us
  starting transfers between devices  23.4 us (43%)
  Pallas kernels  17.6 us (32%)
  waiting for transfers between devices  12.4 us (23%)
  between operations  0.89 us (2%)
    ppermute x12, starting transfers between devices, exchange(): return lax.ppermute(x, 'space', pairs)  23.4 us
    ppermute x12, waiting for transfers between devices, exchange(): return lax.ppermute(x, 'space', pairs)  12.4 us
    pallas_call x1, Pallas kernels, finish(): pl.pallas_call(functools.partial(finish_body, root, out_chunk), in_specs=...  11.5 us
    pallas_call x1, Pallas kernels, local_gram(): pl.pallas_call(functools.partial(gram_body, chunk, part), in_specs=[pl.Bl...  6.09 us
  transfers between devices with their start and end apart: 12, of which 9 were waited for; matrix products, arithmetic and copies ran while one was open for 0% of the time, Pallas kernels for 0%

profile of v3, /device:TPU:1, one launch (start us, length us, event | category | flops | bytes accessed | tf_op | source)
XLA Modules:
  0.0 54.5 jit_solution(13116457690531072086)
XLA Ops:
  0.6 0.0 copy-start.2
  0.6 0.0 copy-start.1
  0.7 0.0 copy-start
  0.7 6.1 %gram.1 = (f32[2,40,128]{2,1,0:T(8,128)S(1)}, f32[2,40,128]{2,1,0:T(8,128)S(1)}, f32[129,16384]{1,0:T(8,128)S(1)}) custom-call(f32[129,16384]{1,0:T(8,128)} %panel_ref.1), custom_call_target="tpu_custom_call" | custom-call | tf_op jit(solution)/shard_map/gram/pallas_call | solution.py:135
  6.8 3.3 %collective-permute-start = (f32[2,40,128]{2,1,0:T(8,128)S(1)}, f32[2,40,128]{2,1,0:T(8,128)S(1)}, u32[]{:S(2)}, u32[]{:S(2)}) collective-permute-start(f32[2,40,128]{2,1,0:T(8,128)S(1)} %get-tuple-element.7), channel_id=1, source_target_pairs={{0,1},{1,0},{2,3},{3,2},{4,5},{5,4},{6,7},{7,6},{8,9},{9,8},{10,11... | collective-permute-start | bytes 122888 | tf_op jit(solution)/shard_map/ppermute | solution.py:154
  10.1 0.9 %collective-permute-done = f32[2,40,128]{2,1,0:T(8,128)S(1)} collective-permute-done((f32[2,40,128]{2,1,0:T(8,128)S(1)}, f32[2,40,128]{2,1,0:T(8,128)S(1)}, u32[]{:S(2)}, u32[]{:S(2)}) %collective-permute-start) | collective-permute-done | bytes 40992 | tf_op jit(solution)/shard_map/ppermute | solution.py:154
  11.0 1.1 %collective-permute-start.3 = (f32[2,40,128]{2,1,0:T(8,128)S(1)}, f32[2,40,128]{2,1,0:T(8,128)S(1)}, u32[]{:S(2)}, u32[]{:S(2)}) collective-permute-start(f32[2,40,128]{2,1,0:T(8,128)S(1)} %pad_maximum_fusion), channel_id=1, source_target_pairs={{0,6},{1,7},{2,4},{3,5},{4,2},{5,3},{6,0},{7,1},{8,14},{9,15},{10,... | collective-permute-start | bytes 122888 | tf_op jit(solution)/shard_map/ppermute | solution.py:154
  12.1 0.4 collective-permute-start.2
  12.4 1.9 %collective-permute-start.1 = (f32[2,40,128]{2,1,0:T(8,128)S(1)}, f32[2,40,128]{2,1,0:T(8,128)S(1)}, u32[]{:S(2)}, u32[]{:S(2)}) collective-permute-start(f32[2,40,128]{2,1,0:T(8,128)S(1)} %pad_maximum_fusion), channel_id=1, source_target_pairs={{0,2},{1,3},{2,0},{3,1},{4,6},{5,7},{6,4},{7,5},{8,10},{9,11},{10,... | collective-permute-start | bytes 122888 | tf_op jit(solution)/shard_map/ppermute | solution.py:154
  14.3 0.8 %collective-permute-done.3 = f32[2,40,128]{2,1,0:T(8,128)S(1)} collective-permute-done((f32[2,40,128]{2,1,0:T(8,128)S(1)}, f32[2,40,128]{2,1,0:T(8,128)S(1)}, u32[]{:S(2)}, u32[]{:S(2)}) %collective-permute-start.3) | collective-permute-done | bytes 40992 | tf_op jit(solution)/shard_map/ppermute | solution.py:154
  15.1 1.3 %collective-permute-done.2 = f32[2,40,128]{2,1,0:T(8,128)S(1)} collective-permute-done((f32[2,40,128]{2,1,0:T(8,128)S(1)}, f32[2,40,128]{2,1,0:T(8,128)S(1)}, u32[]{:S(2)}, u32[]{:S(2)}) %collective-permute-start.2) | collective-permute-done | bytes 40992 | tf_op jit(solution)/shard_map/ppermute | solution.py:154
  16.4 0.0 collective-permute-done.1
  16.5 2.6 %collective-permute-start.6 = (f32[2,40,128]{2,1,0:T(8,128)S(1)}, f32[2,40,128]{2,1,0:T(8,128)S(1)}, u32[]{:S(2)}, u32[]{:S(2)}) collective-permute-start(f32[2,40,128]{2,1,0:T(8,128)S(1)} %pad_maximum_fusion.1), channel_id=1, source_target_pairs={{0,24},{1,25},{2,26},{3,27},{4,28},{5,29},{6,30},{7,31},{8,16},{9,... | collective-permute-start | bytes 122888 | tf_op jit(solution)/shard_map/ppermute | solution.py:154
  19.0 0.5 collective-permute-start.5
  19.6 0.2 collective-permute-start.4
  19.8 0.8 %collective-permute-done.6 = f32[2,40,128]{2,1,0:T(8,128)S(1)} collective-permute-done((f32[2,40,128]{2,1,0:T(8,128)S(1)}, f32[2,40,128]{2,1,0:T(8,128)S(1)}, u32[]{:S(2)}, u32[]{:S(2)}) %collective-permute-start.6) | collective-permute-done | bytes 40992 | tf_op jit(solution)/shard_map/ppermute | solution.py:154
  20.6 2.8 %collective-permute-done.5 = f32[2,40,128]{2,1,0:T(8,128)S(1)} collective-permute-done((f32[2,40,128]{2,1,0:T(8,128)S(1)}, f32[2,40,128]{2,1,0:T(8,128)S(1)}, u32[]{:S(2)}, u32[]{:S(2)}) %collective-permute-start.5) | collective-permute-done | bytes 40992 | tf_op jit(solution)/shard_map/ppermute | solution.py:154
  23.4 0.0 collective-permute-done.4
  23.4 4.4 %collective-permute-start.9 = (f32[2,40,128]{2,1,0:T(8,128)S(1)}, f32[2,40,128]{2,1,0:T(8,128)S(1)}, u32[]{:S(2)}, u32[]{:S(2)}) collective-permute-start(f32[2,40,128]{2,1,0:T(8,128)S(1)} %pad_maximum_fusion.2), channel_id=1, source_target_pairs={{0,96},{1,97},{2,98},{3,99},{4,100},{5,101},{6,102},{7,103},{8,104... | collective-permute-start | bytes 122888 | tf_op jit(solution)/shard_map/ppermute | solution.py:154
  27.9 0.0 collective-permute-start.8
  27.9 0.4 collective-permute-start.7
  28.3 1.0 %collective-permute-done.9 = f32[2,40,128]{2,1,0:T(8,128)S(1)} collective-permute-done((f32[2,40,128]{2,1,0:T(8,128)S(1)}, f32[2,40,128]{2,1,0:T(8,128)S(1)}, u32[]{:S(2)}, u32[]{:S(2)}) %collective-permute-start.9) | collective-permute-done | bytes 40992 | tf_op jit(solution)/shard_map/ppermute | solution.py:154
  29.3 2.6 %collective-permute-done.8 = f32[2,40,128]{2,1,0:T(8,128)S(1)} collective-permute-done((f32[2,40,128]{2,1,0:T(8,128)S(1)}, f32[2,40,128]{2,1,0:T(8,128)S(1)}, u32[]{:S(2)}, u32[]{:S(2)}) %collective-permute-start.8) | collective-permute-done | bytes 40992 | tf_op jit(solution)/shard_map/ppermute | solution.py:154
  31.9 0.0 collective-permute-done.7
  31.9 2.9 %collective-permute-start.10 = (f32[2,40,128]{2,1,0:T(8,128)S(1)}, f32[2,40,128]{2,1,0:T(8,128)S(1)}, u32[]{:S(2)}, u32[]{:S(2)}) collective-permute-start(f32[2,40,128]{2,1,0:T(8,128)S(1)} %pad_maximum_fusion.3), channel_id=1, source_target_pairs={{0,224},{1,225},{2,226},{3,227},{4,228},{5,229},{6,230},{7,231},{8... | collective-permute-start | bytes 122888 | tf_op jit(solution)/shard_map/ppermute | solution.py:154
  34.8 1.4 %collective-permute-done.10 = f32[2,40,128]{2,1,0:T(8,128)S(1)} collective-permute-done((f32[2,40,128]{2,1,0:T(8,128)S(1)}, f32[2,40,128]{2,1,0:T(8,128)S(1)}, u32[]{:S(2)}, u32[]{:S(2)}) %collective-permute-start.10) | collective-permute-done | bytes 40992 | tf_op jit(solution)/shard_map/ppermute | solution.py:154
  36.2 5.7 %collective-permute-start.11 = (f32[2,40,128]{2,1,0:T(8,128)S(1)}, f32[2,40,128]{2,1,0:T(8,128)S(1)}, u32[]{:S(2)}, u32[]{:S(2)}) collective-permute-start(f32[2,40,128]{2,1,0:T(8,128)S(1)} %pad_maximum_fusion.4.mine_ref), channel_id=1, source_target_pairs={{0,1},{1,0},{2,3},{3,2},{4,5},{5,4},{6,7},{7,6},{8,9},{9,8},{10,11... | collective-permute-start | bytes 122888 | tf_op jit(solution)/shard_map/ppermute | solution.py:154
  41.9 0.9 %collective-permute-done.11.other_ref = f32[2,40,128]{2,1,0:T(8,128)S(1)} collective-permute-done((f32[2,40,128]{2,1,0:T(8,128)S(1)}, f32[2,40,128]{2,1,0:T(8,128)S(1)}, u32[]{:S(2)}, u32[]{:S(2)}) %collective-permute-start.11) | collective-permute-done | bytes 40992 | tf_op jit(solution)/shard_map/ppermute | solution.py:154
  42.8 0.0 copy-done.2
  42.8 0.0 copy-done.1
  42.8 0.0 copy-done
  42.8 11.5 %finish.1 = (f32[16,16384]{1,0:T(8,128)}, f32[128,128]{1,0:T(8,128)}, f32[128,128]{1,0:T(8,128)}) custom-call(f32[2,40,128]{2,1,0:T(8,128)S(1)} %pad_maximum_fusion.4.mine_ref, f32[2,40,128]{2,1,0:T(8,128)S(1)} %collective-permute-done.11.other_ref, f32[128,128]{1,0:T(8,128)S(1)} %copy-done, s32[1,16]{1,0:T(1,128)S(1)} %bitcast.2, f32[1,16]{1,0:T(1,128)S(1)} %bitcast.3, ...), custom_call_target="tpu_custom_call" | custom-call | tf_op jit(solution)/shard_map/finish/pallas_call | solution.py:399
  (10 shorter events, 0.1 us)
Async XLA Ops:
  0.6 42.2 %copy-start.2 = (f32[16]{0:T(128)S(1)}, f32[16]{0:T(128)}, u32[]{:S(2)}) copy-start(f32[16]{0:T(128)} %param.7) | copy-start | bytes 196
  0.6 42.2 %copy-start.1 = (s32[16]{0:T(128)S(1)}, s32[16]{0:T(128)}, u32[]{:S(2)}) copy-start(s32[16]{0:T(128)} %param.6) | copy-start | bytes 196
  0.7 42.1 %copy-start = (f32[128,128]{1,0:T(8,128)S(1)}, f32[128,128]{1,0:T(8,128)}, u32[]{:S(2)}) copy-start(f32[128,128]{1,0:T(8,128)} %table_ref.1) | copy-start | bytes 196612
  6.8 4.2 %collective-permute-start = (f32[2,40,128]{2,1,0:T(8,128)S(1)}, f32[2,40,128]{2,1,0:T(8,128)S(1)}, u32[]{:S(2)}, u32[]{:S(2)}) collective-permute-start(f32[2,40,128]{2,1,0:T(8,128)S(1)} %get-tuple-element.7), channel_id=1, source_target_pairs={{0,1},{1,0},{2,3},{3,2},{4,5},{5,4},{6,7},{7,6},{8,9},{9,8},{10,11... | collective-permute-start | bytes 122888 | tf_op jit(solution)/shard_map/ppermute | solution.py:154
  11.0 4.2 %collective-permute-start.3 = (f32[2,40,128]{2,1,0:T(8,128)S(1)}, f32[2,40,128]{2,1,0:T(8,128)S(1)}, u32[]{:S(2)}, u32[]{:S(2)}) collective-permute-start(f32[2,40,128]{2,1,0:T(8,128)S(1)} %pad_maximum_fusion), channel_id=1, source_target_pairs={{0,6},{1,7},{2,4},{3,5},{4,2},{5,3},{6,0},{7,1},{8,14},{9,15},{10,... | collective-permute-start | bytes 122888 | tf_op jit(solution)/shard_map/ppermute | solution.py:154
  12.1 4.4 %collective-permute-start.2 = (f32[2,40,128]{2,1,0:T(8,128)S(1)}, f32[2,40,128]{2,1,0:T(8,128)S(1)}, u32[]{:S(2)}, u32[]{:S(2)}) collective-permute-start(f32[2,40,128]{2,1,0:T(8,128)S(1)} %pad_maximum_fusion), channel_id=1, source_target_pairs={{0,4},{1,5},{2,6},{3,7},{4,0},{5,1},{6,2},{7,3},{8,12},{9,13},{10,... | collective-permute-start | bytes 122888 | tf_op jit(solution)/shard_map/ppermute | solution.py:154
  12.4 4.0 %collective-permute-start.1 = (f32[2,40,128]{2,1,0:T(8,128)S(1)}, f32[2,40,128]{2,1,0:T(8,128)S(1)}, u32[]{:S(2)}, u32[]{:S(2)}) collective-permute-start(f32[2,40,128]{2,1,0:T(8,128)S(1)} %pad_maximum_fusion), channel_id=1, source_target_pairs={{0,2},{1,3},{2,0},{3,1},{4,6},{5,7},{6,4},{7,5},{8,10},{9,11},{10,... | collective-permute-start | bytes 122888 | tf_op jit(solution)/shard_map/ppermute | solution.py:154
  16.5 4.2 %collective-permute-start.6 = (f32[2,40,128]{2,1,0:T(8,128)S(1)}, f32[2,40,128]{2,1,0:T(8,128)S(1)}, u32[]{:S(2)}, u32[]{:S(2)}) collective-permute-start(f32[2,40,128]{2,1,0:T(8,128)S(1)} %pad_maximum_fusion.1), channel_id=1, source_target_pairs={{0,24},{1,25},{2,26},{3,27},{4,28},{5,29},{6,30},{7,31},{8,16},{9,... | collective-permute-start | bytes 122888 | tf_op jit(solution)/shard_map/ppermute | solution.py:154
  19.0 4.4 %collective-permute-start.5 = (f32[2,40,128]{2,1,0:T(8,128)S(1)}, f32[2,40,128]{2,1,0:T(8,128)S(1)}, u32[]{:S(2)}, u32[]{:S(2)}) collective-permute-start(f32[2,40,128]{2,1,0:T(8,128)S(1)} %pad_maximum_fusion.1), channel_id=1, source_target_pairs={{0,16},{1,17},{2,18},{3,19},{4,20},{5,21},{6,22},{7,23},{8,24},{9,... | collective-permute-start | bytes 122888 | tf_op jit(solution)/shard_map/ppermute | solution.py:154
  19.6 3.8 %collective-permute-start.4 = (f32[2,40,128]{2,1,0:T(8,128)S(1)}, f32[2,40,128]{2,1,0:T(8,128)S(1)}, u32[]{:S(2)}, u32[]{:S(2)}) collective-permute-start(f32[2,40,128]{2,1,0:T(8,128)S(1)} %pad_maximum_fusion.1), channel_id=1, source_target_pairs={{0,8},{1,9},{2,10},{3,11},{4,12},{5,13},{6,14},{7,15},{8,0},{9,1},... | collective-permute-start | bytes 122888 | tf_op jit(solution)/shard_map/ppermute | solution.py:154
  23.4 5.8 %collective-permute-start.9 = (f32[2,40,128]{2,1,0:T(8,128)S(1)}, f32[2,40,128]{2,1,0:T(8,128)S(1)}, u32[]{:S(2)}, u32[]{:S(2)}) collective-permute-start(f32[2,40,128]{2,1,0:T(8,128)S(1)} %pad_maximum_fusion.2), channel_id=1, source_target_pairs={{0,96},{1,97},{2,98},{3,99},{4,100},{5,101},{6,102},{7,103},{8,104... | collective-permute-start | bytes 122888 | tf_op jit(solution)/shard_map/ppermute | solution.py:154
  27.9 4.0 %collective-permute-start.8 = (f32[2,40,128]{2,1,0:T(8,128)S(1)}, f32[2,40,128]{2,1,0:T(8,128)S(1)}, u32[]{:S(2)}, u32[]{:S(2)}) collective-permute-start(f32[2,40,128]{2,1,0:T(8,128)S(1)} %pad_maximum_fusion.2), channel_id=1, source_target_pairs={{0,64},{1,65},{2,66},{3,67},{4,68},{5,69},{6,70},{7,71},{8,72},{9,... | collective-permute-start | bytes 122888 | tf_op jit(solution)/shard_map/ppermute | solution.py:154
  27.9 4.0 %collective-permute-start.7 = (f32[2,40,128]{2,1,0:T(8,128)S(1)}, f32[2,40,128]{2,1,0:T(8,128)S(1)}, u32[]{:S(2)}, u32[]{:S(2)}) collective-permute-start(f32[2,40,128]{2,1,0:T(8,128)S(1)} %pad_maximum_fusion.2), channel_id=1, source_target_pairs={{0,32},{1,33},{2,34},{3,35},{4,36},{5,37},{6,38},{7,39},{8,40},{9,... | collective-permute-start | bytes 122888 | tf_op jit(solution)/shard_map/ppermute | solution.py:154
  31.9 4.3 %collective-permute-start.10 = (f32[2,40,128]{2,1,0:T(8,128)S(1)}, f32[2,40,128]{2,1,0:T(8,128)S(1)}, u32[]{:S(2)}, u32[]{:S(2)}) collective-permute-start(f32[2,40,128]{2,1,0:T(8,128)S(1)} %pad_maximum_fusion.3), channel_id=1, source_target_pairs={{0,224},{1,225},{2,226},{3,227},{4,228},{5,229},{6,230},{7,231},{8... | collective-permute-start | bytes 122888 | tf_op jit(solution)/shard_map/ppermute | solution.py:154
  36.2 6.6 %collective-permute-start.11 = (f32[2,40,128]{2,1,0:T(8,128)S(1)}, f32[2,40,128]{2,1,0:T(8,128)S(1)}, u32[]{:S(2)}, u32[]{:S(2)}) collective-permute-start(f32[2,40,128]{2,1,0:T(8,128)S(1)} %pad_maximum_fusion.4.mine_ref), channel_id=1, source_target_pairs={{0,1},{1,0},{2,3},{3,2},{4,5},{5,4},{6,7},{7,6},{8,9},{9,8},{10,11... | collective-permute-start | bytes 122888 | tf_op jit(solution)/shard_map/ppermute | solution.py:154

commit v4 on v3

--- a/solution.py
+++ b/solution.py
@@ -20,6 +20,15 @@
 
 def dot(a, b, dims, precision=None):
     return lax.dot_general(a, b, dims, precision=precision, preferred_element_type=F32)
+
+
+def dot_six(a, b, turn=False):
+    left, right = split3(a), split3(b)
+    order = ((0, 0), (0, 1), (1, 0), (1, 1), (0, 2), (2, 0))
+    stack = jnp.concatenate([left[i] for i, _ in order], axis=1)
+    if turn:
+        return dot(stack, jnp.concatenate([right[j] for _, j in order], axis=1), NT)
+    return dot(stack, jnp.concatenate([right[j] for _, j in order], axis=0), NN)
 
 
 def two_sum(a, b):
@@ -350,15 +359,15 @@
     )
     _, second = factor((s_high + s_low) * column_unscale)
 
-    whole = dot(second, first, NN, HIGH)
+    whole = dot_six(second, first)
     shift_ref[...] = t_high
     z = shift_ref[1:129]
     following = jnp.where(iota((1, 128), 1) == 127, last_unscale, pltpu.roll(unscale, 127, 1))
-    h = dot(whole * (scale * following), z, NN, HIGH)
-    small_ref[1] = dot(second, h, NT, HIGH)
+    h = dot_six(whole * (scale * following), z)
+    small_ref[1] = dot_six(second, h, True)
     operator_out = pltpu.make_async_copy(small_ref.at[1], operator_ref, small_sems.at[1])
     operator_out.start()
-    comb = dot(chosen, whole, NN, HIGH) * scale
+    comb = dot_six(chosen, whole) * scale
 
     shifted = jnp.where(iota(comb.shape, 1) == 0, 0.0, pltpu.roll(comb, 1, 1))
     c = split3(shifted)

time: 54.6 us -> 54.4 us (level)
  no operation moved by 1% of the time
where the time goes in v4:
time: 54.4 us; the launch traced here: 54.3 us
  starting transfers between devices  23.4 us (43%)
  Pallas kernels  17.4 us (32%)
  waiting for transfers between devices  12.4 us (23%)
  between operations  0.89 us (2%)
    ppermute x12, starting transfers between devices, exchange(): return lax.ppermute(x, 'space', pairs)  23.4 us
    ppermute x12, waiting for transfers between devices, exchange(): return lax.ppermute(x, 'space', pairs)  12.4 us
    pallas_call x1, Pallas kernels, finish(): pl.pallas_call(functools.partial(finish_body, root, out_chunk), in_specs=...  11.3 us
    pallas_call x1, Pallas kernels, local_gram(): pl.pallas_call(functools.partial(gram_body, chunk, part), in_specs=[pl.Bl...  6.09 us
  transfers between devices with their start and end apart: 12, of which 9 were waited for; matrix products, arithmetic and copies ran while one was open for 0% of the time, Pallas kernels for 0%

profile of v4, /device:TPU:1, one launch (start us, length us, event | category | flops | bytes accessed | tf_op | source)
XLA Modules:
  0.0 54.3 jit_solution(198350778066269663)
XLA Ops:
  0.6 0.0 copy-start.2
  0.6 0.0 copy-start.1
  0.7 0.0 copy-start
  0.7 6.1 %gram.1 = (f32[2,40,128]{2,1,0:T(8,128)S(1)}, f32[2,40,128]{2,1,0:T(8,128)S(1)}, f32[129,16384]{1,0:T(8,128)S(1)}) custom-call(f32[129,16384]{1,0:T(8,128)} %panel_ref.1), custom_call_target="tpu_custom_call" | custom-call | tf_op jit(solution)/shard_map/gram/pallas_call | solution.py:144
  6.8 3.3 %collective-permute-start = (f32[2,40,128]{2,1,0:T(8,128)S(1)}, f32[2,40,128]{2,1,0:T(8,128)S(1)}, u32[]{:S(2)}, u32[]{:S(2)}) collective-permute-start(f32[2,40,128]{2,1,0:T(8,128)S(1)} %get-tuple-element.7), channel_id=1, source_target_pairs={{0,1},{1,0},{2,3},{3,2},{4,5},{5,4},{6,7},{7,6},{8,9},{9,8},{10,11... | collective-permute-start | bytes 122888 | tf_op jit(solution)/shard_map/ppermute | solution.py:163
  10.1 0.9 %collective-permute-done = f32[2,40,128]{2,1,0:T(8,128)S(1)} collective-permute-done((f32[2,40,128]{2,1,0:T(8,128)S(1)}, f32[2,40,128]{2,1,0:T(8,128)S(1)}, u32[]{:S(2)}, u32[]{:S(2)}) %collective-permute-start) | collective-permute-done | bytes 40992 | tf_op jit(solution)/shard_map/ppermute | solution.py:163
  11.0 1.1 %collective-permute-start.3 = (f32[2,40,128]{2,1,0:T(8,128)S(1)}, f32[2,40,128]{2,1,0:T(8,128)S(1)}, u32[]{:S(2)}, u32[]{:S(2)}) collective-permute-start(f32[2,40,128]{2,1,0:T(8,128)S(1)} %pad_maximum_fusion), channel_id=1, source_target_pairs={{0,6},{1,7},{2,4},{3,5},{4,2},{5,3},{6,0},{7,1},{8,14},{9,15},{10,... | collective-permute-start | bytes 122888 | tf_op jit(solution)/shard_map/ppermute | solution.py:163
  12.1 0.4 collective-permute-start.2
  12.4 1.9 %collective-permute-start.1 = (f32[2,40,128]{2,1,0:T(8,128)S(1)}, f32[2,40,128]{2,1,0:T(8,128)S(1)}, u32[]{:S(2)}, u32[]{:S(2)}) collective-permute-start(f32[2,40,128]{2,1,0:T(8,128)S(1)} %pad_maximum_fusion), channel_id=1, source_target_pairs={{0,2},{1,3},{2,0},{3,1},{4,6},{5,7},{6,4},{7,5},{8,10},{9,11},{10,... | collective-permute-start | bytes 122888 | tf_op jit(solution)/shard_map/ppermute | solution.py:163
  14.3 0.8 %collective-permute-done.3 = f32[2,40,128]{2,1,0:T(8,128)S(1)} collective-permute-done((f32[2,40,128]{2,1,0:T(8,128)S(1)}, f32[2,40,128]{2,1,0:T(8,128)S(1)}, u32[]{:S(2)}, u32[]{:S(2)}) %collective-permute-start.3) | collective-permute-done | bytes 40992 | tf_op jit(solution)/shard_map/ppermute | solution.py:163
  15.1 1.3 %collective-permute-done.2 = f32[2,40,128]{2,1,0:T(8,128)S(1)} collective-permute-done((f32[2,40,128]{2,1,0:T(8,128)S(1)}, f32[2,40,128]{2,1,0:T(8,128)S(1)}, u32[]{:S(2)}, u32[]{:S(2)}) %collective-permute-start.2) | collective-permute-done | bytes 40992 | tf_op jit(solution)/shard_map/ppermute | solution.py:163
  16.4 0.0 collective-permute-done.1
  16.5 2.6 %collective-permute-start.6 = (f32[2,40,128]{2,1,0:T(8,128)S(1)}, f32[2,40,128]{2,1,0:T(8,128)S(1)}, u32[]{:S(2)}, u32[]{:S(2)}) collective-permute-start(f32[2,40,128]{2,1,0:T(8,128)S(1)} %pad_maximum_fusion.1), channel_id=1, source_target_pairs={{0,24},{1,25},{2,26},{3,27},{4,28},{5,29},{6,30},{7,31},{8,16},{9,... | collective-permute-start | bytes 122888 | tf_op jit(solution)/shard_map/ppermute | solution.py:163
  19.0 0.5 collective-permute-start.5
  19.6 0.2 collective-permute-start.4
  19.8 0.8 %collective-permute-done.6 = f32[2,40,128]{2,1,0:T(8,128)S(1)} collective-permute-done((f32[2,40,128]{2,1,0:T(8,128)S(1)}, f32[2,40,128]{2,1,0:T(8,128)S(1)}, u32[]{:S(2)}, u32[]{:S(2)}) %collective-permute-start.6) | collective-permute-done | bytes 40992 | tf_op jit(solution)/shard_map/ppermute | solution.py:163
  20.6 2.8 %collective-permute-done.5 = f32[2,40,128]{2,1,0:T(8,128)S(1)} collective-permute-done((f32[2,40,128]{2,1,0:T(8,128)S(1)}, f32[2,40,128]{2,1,0:T(8,128)S(1)}, u32[]{:S(2)}, u32[]{:S(2)}) %collective-permute-start.5) | collective-permute-done | bytes 40992 | tf_op jit(solution)/shard_map/ppermute | solution.py:163
  23.4 0.0 collective-permute-done.4
  23.4 4.4 %collective-permute-start.9 = (f32[2,40,128]{2,1,0:T(8,128)S(1)}, f32[2,40,128]{2,1,0:T(8,128)S(1)}, u32[]{:S(2)}, u32[]{:S(2)}) collective-permute-start(f32[2,40,128]{2,1,0:T(8,128)S(1)} %pad_maximum_fusion.2), channel_id=1, source_target_pairs={{0,96},{1,97},{2,98},{3,99},{4,100},{5,101},{6,102},{7,103},{8,104... | collective-permute-start | bytes 122888 | tf_op jit(solution)/shard_map/ppermute | solution.py:163
  27.9 0.0 collective-permute-start.8
  27.9 0.4 collective-permute-start.7
  28.3 1.0 %collective-permute-done.9 = f32[2,40,128]{2,1,0:T(8,128)S(1)} collective-permute-done((f32[2,40,128]{2,1,0:T(8,128)S(1)}, f32[2,40,128]{2,1,0:T(8,128)S(1)}, u32[]{:S(2)}, u32[]{:S(2)}) %collective-permute-start.9) | collective-permute-done | bytes 40992 | tf_op jit(solution)/shard_map/ppermute | solution.py:163
  29.3 2.6 %collective-permute-done.8 = f32[2,40,128]{2,1,0:T(8,128)S(1)} collective-permute-done((f32[2,40,128]{2,1,0:T(8,128)S(1)}, f32[2,40,128]{2,1,0:T(8,128)S(1)}, u32[]{:S(2)}, u32[]{:S(2)}) %collective-permute-start.8) | collective-permute-done | bytes 40992 | tf_op jit(solution)/shard_map/ppermute | solution.py:163
  31.9 0.0 collective-permute-done.7
  31.9 2.9 %collective-permute-start.10 = (f32[2,40,128]{2,1,0:T(8,128)S(1)}, f32[2,40,128]{2,1,0:T(8,128)S(1)}, u32[]{:S(2)}, u32[]{:S(2)}) collective-permute-start(f32[2,40,128]{2,1,0:T(8,128)S(1)} %pad_maximum_fusion.3), channel_id=1, source_target_pairs={{0,224},{1,225},{2,226},{3,227},{4,228},{5,229},{6,230},{7,231},{8... | collective-permute-start | bytes 122888 | tf_op jit(solution)/shard_map/ppermute | solution.py:163
  34.8 1.4 %collective-permute-done.10 = f32[2,40,128]{2,1,0:T(8,128)S(1)} collective-permute-done((f32[2,40,128]{2,1,0:T(8,128)S(1)}, f32[2,40,128]{2,1,0:T(8,128)S(1)}, u32[]{:S(2)}, u32[]{:S(2)}) %collective-permute-start.10) | collective-permute-done | bytes 40992 | tf_op jit(solution)/shard_map/ppermute | solution.py:163
  36.2 5.7 %collective-permute-start.11 = (f32[2,40,128]{2,1,0:T(8,128)S(1)}, f32[2,40,128]{2,1,0:T(8,128)S(1)}, u32[]{:S(2)}, u32[]{:S(2)}) collective-permute-start(f32[2,40,128]{2,1,0:T(8,128)S(1)} %pad_maximum_fusion.4.mine_ref), channel_id=1, source_target_pairs={{0,1},{1,0},{2,3},{3,2},{4,5},{5,4},{6,7},{7,6},{8,9},{9,8},{10,11... | collective-permute-start | bytes 122888 | tf_op jit(solution)/shard_map/ppermute | solution.py:163
  41.9 0.9 %collective-permute-done.11.other_ref = f32[2,40,128]{2,1,0:T(8,128)S(1)} collective-permute-done((f32[2,40,128]{2,1,0:T(8,128)S(1)}, f32[2,40,128]{2,1,0:T(8,128)S(1)}, u32[]{:S(2)}, u32[]{:S(2)}) %collective-permute-start.11) | collective-permute-done | bytes 40992 | tf_op jit(solution)/shard_map/ppermute | solution.py:163
  42.8 0.0 copy-done.2
  42.8 0.0 copy-done.1
  42.8 0.0 copy-done
  42.8 11.3 %finish.1 = (f32[16,16384]{1,0:T(8,128)}, f32[128,128]{1,0:T(8,128)}, f32[128,128]{1,0:T(8,128)}) custom-call(f32[2,40,128]{2,1,0:T(8,128)S(1)} %pad_maximum_fusion.4.mine_ref, f32[2,40,128]{2,1,0:T(8,128)S(1)} %collective-permute-done.11.other_ref, f32[128,128]{1,0:T(8,128)S(1)} %copy-done, s32[1,16]{1,0:T(1,128)S(1)} %bitcast.2, f32[1,16]{1,0:T(1,128)S(1)} %bitcast.3, ...), custom_call_target="tpu_custom_call" | custom-call | tf_op jit(solution)/shard_map/finish/pallas_call | solution.py:408
  (10 shorter events, 0.1 us)
Async XLA Ops:
  0.6 42.2 %copy-start.2 = (f32[16]{0:T(128)S(1)}, f32[16]{0:T(128)}, u32[]{:S(2)}) copy-start(f32[16]{0:T(128)} %param.7) | copy-start | bytes 196
  0.6 42.2 %copy-start.1 = (s32[16]{0:T(128)S(1)}, s32[16]{0:T(128)}, u32[]{:S(2)}) copy-start(s32[16]{0:T(128)} %param.6) | copy-start | bytes 196
  0.7 42.1 %copy-start = (f32[128,128]{1,0:T(8,128)S(1)}, f32[128,128]{1,0:T(8,128)}, u32[]{:S(2)}) copy-start(f32[128,128]{1,0:T(8,128)} %table_ref.1) | copy-start | bytes 196612
  6.8 4.2 %collective-permute-start = (f32[2,40,128]{2,1,0:T(8,128)S(1)}, f32[2,40,128]{2,1,0:T(8,128)S(1)}, u32[]{:S(2)}, u32[]{:S(2)}) collective-permute-start(f32[2,40,128]{2,1,0:T(8,128)S(1)} %get-tuple-element.7), channel_id=1, source_target_pairs={{0,1},{1,0},{2,3},{3,2},{4,5},{5,4},{6,7},{7,6},{8,9},{9,8},{10,11... | collective-permute-start | bytes 122888 | tf_op jit(solution)/shard_map/ppermute | solution.py:163
  11.0 4.2 %collective-permute-start.3 = (f32[2,40,128]{2,1,0:T(8,128)S(1)}, f32[2,40,128]{2,1,0:T(8,128)S(1)}, u32[]{:S(2)}, u32[]{:S(2)}) collective-permute-start(f32[2,40,128]{2,1,0:T(8,128)S(1)} %pad_maximum_fusion), channel_id=1, source_target_pairs={{0,6},{1,7},{2,4},{3,5},{4,2},{5,3},{6,0},{7,1},{8,14},{9,15},{10,... | collective-permute-start | bytes 122888 | tf_op jit(solution)/shard_map/ppermute | solution.py:163
  12.1 4.4 %collective-permute-start.2 = (f32[2,40,128]{2,1,0:T(8,128)S(1)}, f32[2,40,128]{2,1,0:T(8,128)S(1)}, u32[]{:S(2)}, u32[]{:S(2)}) collective-permute-start(f32[2,40,128]{2,1,0:T(8,128)S(1)} %pad_maximum_fusion), channel_id=1, source_target_pairs={{0,4},{1,5},{2,6},{3,7},{4,0},{5,1},{6,2},{7,3},{8,12},{9,13},{10,... | collective-permute-start | bytes 122888 | tf_op jit(solution)/shard_map/ppermute | solution.py:163
  12.4 4.0 %collective-permute-start.1 = (f32[2,40,128]{2,1,0:T(8,128)S(1)}, f32[2,40,128]{2,1,0:T(8,128)S(1)}, u32[]{:S(2)}, u32[]{:S(2)}) collective-permute-start(f32[2,40,128]{2,1,0:T(8,128)S(1)} %pad_maximum_fusion), channel_id=1, source_target_pairs={{0,2},{1,3},{2,0},{3,1},{4,6},{5,7},{6,4},{7,5},{8,10},{9,11},{10,... | collective-permute-start | bytes 122888 | tf_op jit(solution)/shard_map/ppermute | solution.py:163
  16.5 4.2 %collective-permute-start.6 = (f32[2,40,128]{2,1,0:T(8,128)S(1)}, f32[2,40,128]{2,1,0:T(8,128)S(1)}, u32[]{:S(2)}, u32[]{:S(2)}) collective-permute-start(f32[2,40,128]{2,1,0:T(8,128)S(1)} %pad_maximum_fusion.1), channel_id=1, source_target_pairs={{0,24},{1,25},{2,26},{3,27},{4,28},{5,29},{6,30},{7,31},{8,16},{9,... | collective-permute-start | bytes 122888 | tf_op jit(solution)/shard_map/ppermute | solution.py:163
  19.0 4.4 %collective-permute-start.5 = (f32[2,40,128]{2,1,0:T(8,128)S(1)}, f32[2,40,128]{2,1,0:T(8,128)S(1)}, u32[]{:S(2)}, u32[]{:S(2)}) collective-permute-start(f32[2,40,128]{2,1,0:T(8,128)S(1)} %pad_maximum_fusion.1), channel_id=1, source_target_pairs={{0,16},{1,17},{2,18},{3,19},{4,20},{5,21},{6,22},{7,23},{8,24},{9,... | collective-permute-start | bytes 122888 | tf_op jit(solution)/shard_map/ppermute | solution.py:163
  19.6 3.8 %collective-permute-start.4 = (f32[2,40,128]{2,1,0:T(8,128)S(1)}, f32[2,40,128]{2,1,0:T(8,128)S(1)}, u32[]{:S(2)}, u32[]{:S(2)}) collective-permute-start(f32[2,40,128]{2,1,0:T(8,128)S(1)} %pad_maximum_fusion.1), channel_id=1, source_target_pairs={{0,8},{1,9},{2,10},{3,11},{4,12},{5,13},{6,14},{7,15},{8,0},{9,1},... | collective-permute-start | bytes 122888 | tf_op jit(solution)/shard_map/ppermute | solution.py:163
  23.4 5.8 %collective-permute-start.9 = (f32[2,40,128]{2,1,0:T(8,128)S(1)}, f32[2,40,128]{2,1,0:T(8,128)S(1)}, u32[]{:S(2)}, u32[]{:S(2)}) collective-permute-start(f32[2,40,128]{2,1,0:T(8,128)S(1)} %pad_maximum_fusion.2), channel_id=1, source_target_pairs={{0,96},{1,97},{2,98},{3,99},{4,100},{5,101},{6,102},{7,103},{8,104... | collective-permute-start | bytes 122888 | tf_op jit(solution)/shard_map/ppermute | solution.py:163
  27.9 4.0 %collective-permute-start.8 = (f32[2,40,128]{2,1,0:T(8,128)S(1)}, f32[2,40,128]{2,1,0:T(8,128)S(1)}, u32[]{:S(2)}, u32[]{:S(2)}) collective-permute-start(f32[2,40,128]{2,1,0:T(8,128)S(1)} %pad_maximum_fusion.2), channel_id=1, source_target_pairs={{0,64},{1,65},{2,66},{3,67},{4,68},{5,69},{6,70},{7,71},{8,72},{9,... | collective-permute-start | bytes 122888 | tf_op jit(solution)/shard_map/ppermute | solution.py:163
  27.9 4.0 %collective-permute-start.7 = (f32[2,40,128]{2,1,0:T(8,128)S(1)}, f32[2,40,128]{2,1,0:T(8,128)S(1)}, u32[]{:S(2)}, u32[]{:S(2)}) collective-permute-start(f32[2,40,128]{2,1,0:T(8,128)S(1)} %pad_maximum_fusion.2), channel_id=1, source_target_pairs={{0,32},{1,33},{2,34},{3,35},{4,36},{5,37},{6,38},{7,39},{8,40},{9,... | collective-permute-start | bytes 122888 | tf_op jit(solution)/shard_map/ppermute | solution.py:163
  31.9 4.3 %collective-permute-start.10 = (f32[2,40,128]{2,1,0:T(8,128)S(1)}, f32[2,40,128]{2,1,0:T(8,128)S(1)}, u32[]{:S(2)}, u32[]{:S(2)}) collective-permute-start(f32[2,40,128]{2,1,0:T(8,128)S(1)} %pad_maximum_fusion.3), channel_id=1, source_target_pairs={{0,224},{1,225},{2,226},{3,227},{4,228},{5,229},{6,230},{7,231},{8... | collective-permute-start | bytes 122888 | tf_op jit(solution)/shard_map/ppermute | solution.py:163
  36.2 6.6 %collective-permute-start.11 = (f32[2,40,128]{2,1,0:T(8,128)S(1)}, f32[2,40,128]{2,1,0:T(8,128)S(1)}, u32[]{:S(2)}, u32[]{:S(2)}) collective-permute-start(f32[2,40,128]{2,1,0:T(8,128)S(1)} %pad_maximum_fusion.4.mine_ref), channel_id=1, source_target_pairs={{0,1},{1,0},{2,3},{3,2},{4,5},{5,4},{6,7},{7,6},{8,9},{9,8},{10,11... | collective-permute-start | bytes 122888 | tf_op jit(solution)/shard_map/ppermute | solution.py:163
